TPU v7x, 128 devices: a whole 4x4x4 slice. The times are simulated.
128 devices in a mesh: dp: 128 (over z, y, x, core).
Axes of the slice: x: 4, y: 4, z: 4, core: 2. Of those that a mesh axis runs over, the one named last changes fastest.
Arguments:
- text_states: bfloat16 [2048, 16, 768], P('dp'), may hold values from -6 to 6
- text_len: int32 [2048], P('dp'), may hold values from 1 to 16
- query_states: bfloat16 [2048, 16, 768], P('dp'), may hold values from -6 to 6
- neg_owner: int32 [2048, 2], P('dp'), may hold values from 0 to 127, all different within a row; in each aligned block of 16 rows (0 to 15, 16 to 31, ...) at most 2 rows name the same one
- neg_slot: int32 [2048, 2], P('dp'), may hold values from 0 to 15
- projection_weight: bfloat16 [768, 2304], replicated, may hold values from -0.21875 to 0.21875
- output_weight: bfloat16 [768, 768], replicated, may hold values from -0.21875 to 0.21875
- ln_gain: float32 [768], replicated, may hold values from 0.5 to 1.5
- ln_bias: float32 [768], replicated, may hold values from -3 to 3
- itm_weight: float32 [768, 2], replicated, may hold values from -0.875 to 0.875
- itm_bias: float32 [2], replicated, may hold values from -3 to 3
Outputs:
- pair_logits: float32 [2048, 3, 2], P('dp')
- grad_text: bfloat16 [2048, 16, 768], P('dp')
- grad_query: bfloat16 [2048, 16, 768], P('dp')
- grad_qkv: float32 [768, 2304], replicated
- grad_out: float32 [768, 768], replicated
Inputs may be any that keep to these rules, and one draw needn't show every extreme that they name: `neg_owner`: the two negatives of a caption lie in different blocks; among the 16 captions of one device no block is named more than 2 times, and in some device exactly 2 times.
All inputs are finite; a program needn't handle non-finite values.
Results may differ from a plain program's by a relative error of at most 0.0075.
Values may be sent and summed in bfloat16 or wider, within the bound.
A program may use at most 128 MiB of HBM per device.

v0:
```python
import math

import jax
import jax.numpy as jnp
from jax import lax
from jax.sharding import PartitionSpec as P

HEADS = 12
CAP = 2


def matrix_product(einsum_form, left_side, right_side):
    return jnp.einsum(einsum_form, left_side, right_side, preferred_element_type=jnp.float32)


def split_heads(tensor, head_number):
    return tensor.reshape(tensor.shape[:-1] + (head_number, tensor.shape[-1] // head_number))


def merge_heads(tensor):
    return tensor.reshape(tensor.shape[0], tensor.shape[1], tensor.shape[2] * tensor.shape[3])


def tail_loss(hidden_states, ln_gain, ln_bias, itm_weight, itm_bias, labels):
    center = hidden_states - jnp.mean(hidden_states, axis=-1, keepdims=True)
    spread = jnp.mean(center * center, axis=-1, keepdims=True)
    normed = center * lax.rsqrt(spread + 1e-06) * ln_gain + ln_bias
    pooled = jnp.mean(normed, axis=1)
    logits = jnp.dot(pooled, itm_weight, precision=lax.Precision.HIGHEST) + itm_bias
    losses = jax.nn.logsumexp(logits, axis=-1) - jnp.sum(logits * labels, axis=-1)
    return (jnp.sum(losses), logits)


def pair_work(
    caption_rows,
    lengths,
    images,
    projection_weight,
    output_weight,
    ln_gain,
    ln_bias,
    itm_weight,
    itm_bias,
):
    caption_texts, text_rows, hidden_width = caption_rows.shape
    query_row_count = images.shape[2]
    pair_rows = caption_texts * 3
    head_number = HEADS
    score_scale = 1.0 / math.sqrt(hidden_width // head_number)
    text_kv = matrix_product(
        "bld,de->ble", caption_rows, projection_weight[:, hidden_width:]
    ).astype(jnp.bfloat16)
    image_row_count = images.reshape(pair_rows, query_row_count, hidden_width)
    image_projected = matrix_product("tns,sm->tnm", image_row_count, projection_weight).astype(
        jnp.bfloat16
    )
    text_wide = jnp.broadcast_to(
        text_kv[:, None], (caption_texts, 3, text_rows, 2 * hidden_width)
    ).reshape(pair_rows, text_rows, 2 * hidden_width)
    queries = split_heads(image_projected[:, :, :hidden_width], head_number)
    key_heads = split_heads(
        jnp.concatenate(
            [
                image_projected[:, :, hidden_width : 2 * hidden_width],
                text_wide[:, :, :hidden_width],
            ],
            axis=1,
        ),
        head_number,
    )
    value_heads = split_heads(
        jnp.concatenate(
            [image_projected[:, :, 2 * hidden_width :], text_wide[:, :, hidden_width:]], axis=1
        ),
        head_number,
    )
    position = jnp.arange(query_row_count + text_rows)
    key_valid = (position[None, :] < query_row_count) | (
        position[None, :] - query_row_count < lengths[:, None]
    )
    key_valid = jnp.repeat(key_valid, 3, axis=0)
    scores = matrix_product("bqhe,bkhe->bhqk", queries, key_heads) * score_scale
    scores = jnp.where(key_valid[:, None, None, :], scores, -1e30)
    shifted = jnp.exp(scores - jnp.max(scores, axis=-1, keepdims=True))
    weights = shifted / jnp.sum(shifted, axis=-1, keepdims=True)
    weights_low = weights.astype(jnp.bfloat16)
    attended_context = merge_heads(
        matrix_product("bhqk,bkhe->bqhe", weights_low, value_heads).astype(jnp.bfloat16)
    )
    hidden_states = image_row_count.astype(jnp.float32) + matrix_product(
        "tns,sm->tnm", attended_context, output_weight
    )
    labels = jnp.tile(
        jnp.array([[0.0, 1.0], [1.0, 0.0], [1.0, 0.0]], dtype=jnp.float32), (caption_texts, 1)
    )

    def loss_of(hidden_in):
        return tail_loss(hidden_in, ln_gain, ln_bias, itm_weight, itm_bias, labels)

    loss_total, pullback, logits = jax.vjp(loss_of, hidden_states, has_aux=True)
    hidden_gradient = pullback(jnp.ones_like(loss_total))[0]
    attention_gradient = hidden_gradient.astype(jnp.bfloat16)
    output_weight_gradient = matrix_product("nxv,nxl->vl", attended_context, attention_gradient)
    return (
        logits,
        attended_context,
        attention_gradient,
        hidden_gradient,
        output_weight_gradient,
        image_row_count,
        queries,
        key_heads,
        value_heads,
        weights,
        weights_low,
    )


def pair_backward(
    caption_rows,
    projection_weight,
    output_weight,
    query_row_count,
    attention_gradient,
    hidden_gradient,
    queries,
    key_heads,
    value_heads,
    weights,
    weights_low,
):
    caption_texts, text_rows, hidden_width = caption_rows.shape
    head_number = HEADS
    score_scale = 1.0 / math.sqrt(hidden_width // head_number)
    context_gradient = split_heads(
        matrix_product("kvp,mp->kvm", attention_gradient, output_weight).astype(jnp.bfloat16),
        head_number,
    )
    grad_probs = matrix_product("bqhe,bkhe->bhqk", context_gradient, value_heads)
    grad_values = matrix_product("bhqk,bqhe->bkhe", weights_low, context_gradient)
    grad_scores = (
        weights * (grad_probs - jnp.sum(grad_probs * weights, axis=-1, keepdims=True)) * score_scale
    ).astype(jnp.bfloat16)
    grad_queries = merge_heads(matrix_product("bhqk,bkhe->bqhe", grad_scores, key_heads))
    grad_keys = merge_heads(matrix_product("bhqk,bqhe->bkhe", grad_scores, queries))
    grad_values = merge_heads(grad_values)
    image_projection_gradient = jnp.concatenate(
        [grad_queries, grad_keys[:, :query_row_count], grad_values[:, :query_row_count]], axis=-1
    ).astype(jnp.bfloat16)
    grad_text_kv = jnp.concatenate(
        [grad_keys[:, query_row_count:], grad_values[:, query_row_count:]], axis=-1
    )
    grad_text_kv = jnp.sum(
        grad_text_kv.reshape(caption_texts, 3, text_rows, 2 * hidden_width), axis=1
    ).astype(jnp.bfloat16)
    image_gradient = (
        matrix_product("kvp,mp->kvm", image_projection_gradient, projection_weight)
        + hidden_gradient
    ).reshape(caption_texts, 3, query_row_count, hidden_width)
    grad_text = matrix_product("ble,de->bld", grad_text_kv, projection_weight[:, hidden_width:])
    return (grad_text, image_gradient, image_projection_gradient, grad_text_kv)


def on_device(
    text_states,
    text_len,
    query_states,
    neg_owner,
    neg_slot,
    projection_weight,
    output_weight,
    ln_gain,
    ln_bias,
    itm_weight,
    itm_bias,
):
    caption_count = text_states.shape[0]
    query_row_count = query_states.shape[1]
    hidden_width = query_states.shape[2]
    peer_count = lax.axis_size("dp")
    capacity = CAP
    flat_owner = neg_owner.reshape(-1)
    flat_slot = neg_slot.reshape(-1)
    request_count = flat_owner.shape[0]
    request_ids = jnp.arange(request_count)
    same_owner = flat_owner[:, None] == flat_owner[None, :]
    before = request_ids[:, None] > request_ids[None, :]
    rank_within = jnp.sum((same_owner & before).astype(jnp.int32), axis=1)
    bucket = flat_owner * capacity + rank_within
    slot_hot = bucket[:, None] == jnp.arange(peer_count * capacity)[None, :]
    wanted = jnp.sum(jnp.where(slot_hot, flat_slot[:, None] + 1, 0), axis=0).reshape(
        peer_count, capacity
    )
    requested = lax.all_to_all(wanted, "dp", split_axis=0, concat_axis=0, tiled=True)
    send_select = (requested.reshape(-1)[:, None] == jnp.arange(caption_count)[None, :] + 1).astype(
        jnp.bfloat16
    )
    outgoing = jnp.dot(
        send_select, query_states.reshape(caption_count, -1), preferred_element_type=jnp.float32
    ).astype(jnp.bfloat16)
    outgoing = outgoing.reshape(peer_count, capacity, query_row_count, hidden_width)
    fetched = lax.all_to_all(outgoing, "dp", split_axis=0, concat_axis=0, tiled=True)
    take_select = slot_hot.astype(jnp.bfloat16)
    negatives = jnp.dot(
        take_select, fetched.reshape(peer_count * capacity, -1), preferred_element_type=jnp.float32
    ).astype(jnp.bfloat16)
    negatives = negatives.reshape(caption_count, 2, query_row_count, hidden_width)
    images = jnp.concatenate([query_states[:, None], negatives], axis=1)
    (
        logits,
        attended_context,
        attention_gradient,
        hidden_gradient,
        output_weight_gradient,
        image_row_count,
        queries,
        key_heads,
        value_heads,
        weights,
        weights_low,
    ) = pair_work(
        text_states,
        text_len,
        images,
        projection_weight,
        output_weight,
        ln_gain,
        ln_bias,
        itm_weight,
        itm_bias,
    )
    all_pairs = caption_count * peer_count
    grad_text, image_gradient, image_projection_gradient, grad_text_kv = pair_backward(
        text_states,
        projection_weight,
        output_weight,
        query_row_count,
        attention_gradient,
        hidden_gradient,
        queries,
        key_heads,
        value_heads,
        weights,
        weights_low,
    )
    back_rows = image_gradient[:, 1:].astype(jnp.bfloat16).reshape(request_count, -1)
    outgoing_grads = jnp.dot(take_select.T, back_rows, preferred_element_type=jnp.float32).astype(
        jnp.bfloat16
    )
    outgoing_grads = outgoing_grads.reshape(peer_count, capacity, query_row_count, hidden_width)
    returned = lax.all_to_all(outgoing_grads, "dp", split_axis=0, concat_axis=0, tiled=True)
    projection_weight_gradient = matrix_product(
        "nxv,nxl->vl", image_row_count, image_projection_gradient
    )
    projection_weight_gradient = projection_weight_gradient + jnp.pad(
        matrix_product("bld,ble->de", text_states, grad_text_kv), ((0, 0), (hidden_width, 0))
    )
    sum_qkv, sum_out = lax.psum((projection_weight_gradient, output_weight_gradient), "dp")
    received = jnp.dot(
        send_select.T,
        returned.reshape(peer_count * capacity, -1),
        preferred_element_type=jnp.float32,
    )
    grad_query = (
        image_gradient[:, 0] + received.reshape(caption_count, query_row_count, hidden_width)
    ).astype(jnp.bfloat16)
    return (
        logits.reshape(caption_count, 3, 2),
        grad_text.astype(jnp.bfloat16),
        grad_query,
        sum_qkv / all_pairs,
        sum_out / all_pairs,
    )


def solution(mesh):
    placed = (
        P("dp", None, None),
        P("dp"),
        P("dp", None, None),
        P("dp", None),
        P("dp", None),
        P(),
        P(),
        P(),
        P(),
        P(),
        P(),
    )
    return jax.shard_map(
        on_device,
        mesh=mesh,
        in_specs=placed,
        out_specs=(P("dp", None, None), P("dp", None, None), P("dp", None, None), P(), P()),
        check_vma=False,
    )
```

profile of v0, /device:TPU:1, one launch (start us, length us, event | category | flops | bytes accessed | tf_op | source)
XLA Modules:
  0.0 793.7 jit_solution(434078617493572665)
XLA Ops:
  10.1 11.5 %all-to-all-start = ((s32[128,1,2]{2,1,0:T(1,128)}), s32[128,1,2]{2,1,0:T(1,128)S(1)}, u32[]{:S(2)}, u32[]{:S(2)}) async-start(s32[128,1,2]{2,1,0:T(1,128)} %bitcast.2), calls=%async_computation | async-start | bytes 131072 | tf_op jit(solution)/shard_map/all_to_all | solution.py:194
  22.7 8.4 %all-to-all-done = s32[128,1,2]{2,1,0:T(1,128)S(1)} async-done(((s32[128,1,2]{2,1,0:T(1,128)}), s32[128,1,2]{2,1,0:T(1,128)S(1)}, u32[]{:S(2)}, u32[]{:S(2)}) %all-to-all-start) | async-done | bytes 1056 | tf_op jit(solution)/shard_map/all_to_all | solution.py:194
  34.5 4.6 copy.107
  39.1 6.0 all-to-all-start.1
  49.7 70.6 %all-to-all-done.1 = bf16[128,2,16,768]{3,2,1,0:T(8,128)(2,1)} async-done(((bf16[128,2,16,768]{3,2,1,0:T(8,128)(2,1)}), bf16[128,2,16,768]{3,2,1,0:T(8,128)(2,1)}, u32[]{:S(2)}, u32[]{:S(2)}) %all-to-all-start.1) | async-done | bytes 6291488 | tf_op jit(solution)/shard_map/all_to_all | solution.py:202
  120.3 5.6 copy.108
  136.4 8.2 %reshape.168 = bf16[48,32,12,64]{3,2,1,0:T(8,128)(2,1)} reshape(bf16[48,32,768]{2,1,0:T(8,128)(2,1)} %get-tuple-element.38) | data formatting | bytes 4718592 | tf_op jit(solution)/shard_map/reshape | solution.py:17
  144.6 4.7 reshape.167
  149.3 5.9 reshape.166
  155.2 6.3 fusion.15
  161.5 97.7 %fusion.80 = (f32[48,12,16]{2,1,0:T(8,128)S(1)}, f32[48,12,16,32]{3,2,1,0:T(8,128)S(1)}) fusion(f32[48,12,16,32]{3,2,1,0:T(8,128)S(1)} %fusion.15, pred[48,32]{1,0:T(8,128)(4,1)S(1)} %broadcast_in_dim.85), kind=kOutput, calls=%fused_computation.125 | output fusion | flops 1769503 | bytes 2397696 | tf_op jit(solution)/shard_map/sub | solution.py:84
  264.0 15.2 %reshape.169 = bf16[48,16,768]{2,1,0:T(8,128)(2,1)} reshape(bf16[48,16,12,64]{3,2,1,0:T(8,128)(2,1)} %copy.89) | data formatting | bytes 2359296 | tf_op jit(solution)/shard_map/reshape | solution.py:21
  288.6 4.7 reshape.171
  293.3 8.6 %fusion.9 = f32[48,12,16,32]{3,2,1,0:T(8,128)} fusion(bf16[48,32,12,64]{3,2,1,0:T(8,128)(2,1)} %reshape.166, bf16[48,16,12,64]{3,2,1,0:T(8,128)(2,1)} %reshape.171), kind=kOutput, calls=%fused_computation.25 | convolution fusion | flops 37748736 | bytes 4718592 | tf_op jit(solution)/shard_map/bqhe,bkhe->bhqk/dot_general | solution.py:13
  301.9 57.1 %convert_bitcast_fusion = bf16[48,16,12,64]{3,1,2,0:T(8,128)(2,1)} fusion(bf16[48,32,12,64]{3,2,1,0:T(8,128)(2,1)} %reshape.168, f32[48,12,16,32]{3,2,1,0:T(8,128)} %fusion.9, f32[48,12,16,32]{3,2,1,0:T(8,128)} %copy-done.38, f32[48,12,16]{2,1,0:T(8,128)S(1)} %copy-done.40), kind=kOutput, calls=%fused_computation.42 | convolution fusion | flops 40412192 | bytes 5935104 | tf_op jit(solution)/shard_map/bhqk,bkhe->bqhe/dot_general | solution.py:13
  359.0 61.1 %convolution_bitcast_fusion.2 = f32[48,32,12,64]{3,1,2,0:T(8,128)} fusion(bf16[48,16,12,64]{3,2,1,0:T(8,128)(2,1)} %reshape.167, f32[48,12,16,32]{3,2,1,0:T(8,128)} %fusion.9, f32[48,12,16,32]{3,2,1,0:T(8,128)} %copy-done.38, f32[48,12,16]{2,1,0:T(8,128)S(1)} %copy-done.40), kind=kOutput, calls=%fused_computation.22 | convolution fusion | flops 39822368 | bytes 8294400 | tf_op jit(solution)/shard_map/bhqk,bqhe->bkhe/dot_general | solution.py:13
  420.1 10.9 %convolution_bitcast_fusion.1 = f32[48,32,12,64]{3,1,2,0:T(8,128)} fusion(bf16[48,16,12,64]{3,2,1,0:T(8,128)(2,1)} %reshape.171, f32[48,12,16,32]{3,2,1,0:T(8,128)} %copy-done.38, f32[48,12,16]{2,1,0:T(8,128)S(1)} %copy-done.40), kind=kOutput, calls=%fused_computation.21 | convolution fusion | flops 38338560 | bytes 7114752 | tf_op jit(solution)/shard_map/bhqk,bqhe->bkhe/dot_general | solution.py:13
  431.0 13.4 %copy.93 = f32[48,32,12,64]{3,2,1,0:T(8,128)} copy(f32[48,32,12,64]{3,1,2,0:T(8,128)S(1)} %copy-done.3) | data formatting | bytes 9437184 | tf_op jit(solution)/shard_map/bhqk,bqhe->bkhe/transpose | solution.py:13
  444.4 9.9 %reshape.172 = f32[48,32,768]{2,1,0:T(8,128)} reshape(f32[48,32,12,64]{3,2,1,0:T(8,128)} %copy.93) | data formatting | bytes 9437184 | tf_op jit(solution)/shard_map/reshape | solution.py:21
  460.5 17.0 %copy.95 = f32[48,32,12,64]{3,2,1,0:T(8,128)} copy(f32[48,32,12,64]{3,1,2,0:T(8,128)} %convolution_bitcast_fusion.1) | data formatting | bytes 9437184 | tf_op jit(solution)/shard_map/bhqk,bqhe->bkhe/transpose | solution.py:13
  477.5 10.1 %reshape.173 = f32[48,32,768]{2,1,0:T(8,128)} reshape(f32[48,32,12,64]{3,2,1,0:T(8,128)} %copy.95) | data formatting | bytes 9437184 | tf_op jit(solution)/shard_map/reshape | solution.py:21
  496.3 4.7 reshape.175
  501.1 5.2 pad_maximum_fusion
  511.4 5.2 add_add_fusion.1
  516.6 5.6 bitcast_add_fusion
  524.8 4.5 copy.111
  529.2 5.9 all-to-all-start.2
  544.8 209.8 %all-reduce.4.cloned.1.call-done = (f32[768,2304]{1,0:T(8,128)}, f32[768,768]{1,0:T(8,128)}) async-done(((f32[768,2304]{1,0:T(8,128)}, f32[768,768]{1,0:T(8,128)}), (f32[768,2304]{1,0:T(8,128)}, f32[768,768]{1,0:T(8,128)})) %all-reduce.4.cloned.1.call-update) | async-done | bytes 9437200 | tf_op jit(solution)/shard_map/psum | solution.py:258
  757.8 6.4 broadcast_multiply_fusion
  764.2 8.2 %copy.112 = bf16[32,8,16,768]{3,1,2,0:T(8,128)(2,1)} copy(bf16[32,8,16,768]{3,2,1,0:T(8,128)(2,1)} %bitcast.45) | data formatting | bytes 12582912
  772.4 8.6 %copy.99 = bf16[256,12288]{0,1:T(8,128)(2,1)} copy(bf16[256,12288]{1,0:T(8,128)(2,1)} %bitcast.97) | data formatting | bytes 12582912 | tf_op jit(solution)/shard_map/reshape | solution.py:261
  781.0 4.6 fusion.40
  (150 shorter events, 72.5 us)
Async XLA Ops:
  7.2 272.0 %copy-start = (bf16[768,768]{1,0:T(8,128)(2,1)S(1)}, bf16[768,768]{1,0:T(8,128)(2,1)}, u32[]{:S(2)}) copy-start(bf16[768,768]{1,0:T(8,128)(2,1)} %param.18) | copy-start | bytes 3538948
  8.3 117.6 %copy-start.29 = (s32[32]{0:T(128)}, s32[32]{0:T(128)S(1)}, u32[]{:S(2)}) copy-start(s32[32]{0:T(128)S(1)} %multiply_add_fusion.1) | copy-start | bytes 388
  10.1 21.0 %all-to-all-start = ((s32[128,1,2]{2,1,0:T(1,128)}), s32[128,1,2]{2,1,0:T(1,128)S(1)}, u32[]{:S(2)}, u32[]{:S(2)}) async-start(s32[128,1,2]{2,1,0:T(1,128)} %bitcast.2), calls=%async_computation | async-start | bytes 131072 | tf_op jit(solution)/shard_map/all_to_all | solution.py:194
  21.6 12.9 %copy-start.31 = (s32[16]{0:T(128)}, s32[16]{0:T(128)S(1)}, u32[]{:S(2)}) copy-start(s32[16]{0:T(128)S(1)} %iota_add_fusion.1) | copy-start | bytes 196
  39.1 6.0 copy-start.36
  39.1 6.2 copy-start.34
  39.1 6.3 copy-start.18
  39.1 81.2 %all-to-all-start.1 = ((bf16[128,2,16,768]{3,2,1,0:T(8,128)(2,1)}), bf16[128,2,16,768]{3,2,1,0:T(8,128)(2,1)}, u32[]{:S(2)}, u32[]{:S(2)}) async-start(bf16[128,2,16,768]{3,2,1,0:T(8,128)(2,1)} %bitcast.94), calls=%async_computation.1 | async-start | bytes 12582912 | tf_op jit(solution)/shard_map/all_to_all | solution.py:202
  127.1 2.4 copy-start.37
  161.5 97.7 %copy-start.2 = (bf16[48,32,12,64]{3,2,1,0:T(8,128)(2,1)S(1)}, bf16[48,32,12,64]{3,2,1,0:T(8,128)(2,1)}, u32[]{:S(2)}) copy-start(bf16[48,32,12,64]{3,2,1,0:T(8,128)(2,1)} %reshape.166) | copy-start | bytes 7077892
  259.2 2.2 copy-start.38
  259.2 2.3 copy-start.39
  282.1 3.5 copy-start.16
  282.7 2.8 copy-start.19
  293.3 8.6 %copy-start.40 = (f32[48,12,16]{2,1,0:T(8,128)S(1)}, f32[48,12,16]{2,1,0:T(8,128)}, u32[]{:S(2)}) copy-start(f32[48,12,16]{2,1,0:T(8,128)} %copy-done.39) | copy-start | bytes 110596
  420.1 10.9 %copy-start.3 = (f32[48,32,12,64]{3,1,2,0:T(8,128)S(1)}, f32[48,32,12,64]{3,1,2,0:T(8,128)}, u32[]{:S(2)}) copy-start(f32[48,32,12,64]{3,1,2,0:T(8,128)} %convolution_bitcast_fusion.2) | copy-start | bytes 14155780
  487.6 6.2 copy-start.6
  509.2 2.1 copy-start.9
  509.2 2.1 copy-start.12
  509.2 2.1 copy-start.13
  509.3 2.2 copy-start.14
  509.3 2.1 copy-start.17
  509.3 2.1 copy-start.20
  509.3 2.1 copy-start.22
  509.3 2.1 copy-start.26
  511.4 5.2 copy-start.11
  516.6 5.7 copy-start.15
  529.2 235.0 %all-to-all-start.2 = ((bf16[128,2,16,768]{3,2,1,0:T(8,128)(2,1)}), bf16[128,2,16,768]{3,2,1,0:T(8,128)(2,1)}, u32[]{:S(2)}, u32[]{:S(2)}) async-start(bf16[128,2,16,768]{3,2,1,0:T(8,128)(2,1)} %bitcast.93), calls=%async_computation.2 | async-start | bytes 12582912 | tf_op jit(solution)/shard_map/all_to_all | solution.py:251
  535.1 219.5 %all-reduce.4.cloned.1.call-start = ((), (), s32[]{:S(2)}) async-start(), calls=%async_computation.3 | async-start | bytes 18874368 | tf_op jit(solution)/shard_map/psum | solution.py:258
  772.4 8.6 %copy-start.28 = (s32[256]{0:T(256)S(1)}, s32[256]{0:T(256)}, u32[]{:S(2)}) copy-start(s32[256]{0:T(256)} %copy-done.27) | copy-start | bytes 3076
  772.4 8.6 %copy-start.32 = (s32[16]{0:T(128)S(1)}, s32[16]{0:T(128)}, u32[]{:S(2)}) copy-start(s32[16]{0:T(128)} %copy-done.31) | copy-start | bytes 196
  781.0 5.5 copy-start.1
  (13 other events, 15.4 us)
Sparse Core Ops, SparseCore 0:
  541.6 212.9 all-reduce.3
where the time goes:
time: 800 us; the launch traced here: 794 us
  waiting for transfers between devices  289 us (36%)
  matrix products  187 us (23%)
  local copies, waits for them, and re-layouts  157 us (20%)
  other arithmetic  122 us (15%)
  starting transfers between devices  23.7 us (3%)
  between operations  15 us (2%)
    psum x1, waiting for transfers between devices, on_device(): lax.psum((projection_weight_gradient, output_weight_gradient), 'dp')  210 us
    dot_general x15, matrix products, matrix_product(): jnp.einsum(einsum_form, left_side, right_side, preferred_element_type=jnp...  177 us
    sub x1, other arithmetic, pair_work(): shifted = jnp.exp(scores - jnp.max(scores, axis=-1, keepdims=True))  97.7 us
    all_to_all x1, waiting for transfers between devices, on_device(): lax.all_to_all(outgoing, 'dp', split_axis=0, concat_axis=0, tiled=True)  70.6 us
    reshape x4, local copies, waits for them, and re-layouts, merge_heads(): tensor.reshape(tensor.shape[0], tensor.shape[1], tensor.shape[2] * tensor...  40.1 us
    transpose x3, local copies, waits for them, and re-layouts, matrix_product(): jnp.einsum(einsum_form, left_side, right_side, preferred_element_type=jnp...  32.9 us
    unnamed x92, local copies, waits for them, and re-layouts  31 us
    reshape x4, local copies, waits for them, and re-layouts, split_heads(): tensor.reshape(tensor.shape[:-1] + (head_number, tensor.shape[-1] // head...  23.4 us
  transfers between devices with their start and end apart: 4, of which 3 were waited for; matrix products, arithmetic and copies ran while one was open for 3% of the time, Pallas kernels for 0%

commit v1 on v0

v1 whole, which is shorter than its diff:
```python
import math
import jax
import jax.numpy as jnp
from jax import lax
from jax.experimental import pallas as pl
from jax.experimental.pallas import tpu as pltpu
from jax.sharding import PartitionSpec as P

CAP = 2
F32 = jnp.float32
BF = jnp.bfloat16
NN = (((1,), (0,)), ((), ()))
NT = (((1,), (1,)), ((), ()))
TN = (((0,), (0,)), ((), ()))


def mm(a, b, dims):
    return lax.dot_general(a, b, dims, preferred_element_type=F32)


def attention_kernel(
    lens, ibias, x_ref, t_ref, w_ref, wo_ref, gain_ref, bias_ref, iw_ref,
    logits_ref, gtext_ref, own_ref, neg_ref, dw_ref, dwo_ref,
    qkv, tkv, ctx, gh, ga, gc, gqkv, gt, prob,
):
    rows, width = x_ref.shape
    trows = t_ref.shape[0]
    pairs_of_heads = width // 128
    unit = 96
    units = rows // unit
    scale = 1.0 / math.sqrt(64.0)
    col = 256

    def qkv_step(j, _):
        c = pl.ds(pl.multiple_of(j * col, col), col)
        qkv[:, c] = mm(x_ref[...], w_ref[:, c], NN).astype(BF)
        return 0

    lax.fori_loop(0, 3 * width // col, qkv_step, 0)

    def tkv_step(j, _):
        c = pl.ds(pl.multiple_of(j * col, col), col)
        cw = pl.ds(pl.multiple_of(j * col + width, col), col)
        tkv[:, c] = mm(t_ref[...], w_ref[:, cw], NN).astype(BF)
        return 0

    lax.fori_loop(0, 2 * width // col, tkv_step, 0)

    lane = lax.broadcasted_iota(jnp.int32, (1, 128), 1)
    low = lane < 64

    def by_head(a):
        zero = jnp.zeros_like(a)
        return jnp.concatenate([jnp.where(low, a, zero), jnp.where(low, zero, a)], axis=0)

    def keys_of(g, j, first):
        r = pl.ds(pl.multiple_of(g * unit, 32), unit)
        tr = pl.ds(pl.multiple_of(g * 32, 32), 32)
        image = qkv[r, first + j * 128 : first + (j + 1) * 128]
        text = tkv[tr, first - width + j * 128 : first - width + (j + 1) * 128]
        return by_head(jnp.concatenate([image, text], axis=0))

    def forward(g, _):
        r = pl.ds(pl.multiple_of(g * unit, 32), unit)
        rowi = lax.broadcasted_iota(jnp.int32, (unit, 128), 0)
        lanei = lax.broadcasted_iota(jnp.int32, (unit, 128), 1)
        first = rowi < 48
        start = jnp.where(first, 96, 112)
        live = jnp.where(first, lens[2 * g], lens[2 * g + 1])
        block = rowi - lax.rem(rowi, 16)
        valid = ((lanei >= block) & (lanei < block + 16)) | ((lanei >= start) & (lanei < start + live))
        for j in range(pairs_of_heads):
            q = qkv[r, j * 128 : (j + 1) * 128]
            s = mm(q, keys_of(g, j, width), NT) * scale
            parts = []
            for h in range(2):
                sh = jnp.where(valid, s[:, h * 128 : (h + 1) * 128], -1e30)
                e = jnp.exp(sh - jnp.max(sh, axis=-1, keepdims=True))
                parts.append(e / jnp.sum(e, axis=-1, keepdims=True))
            p = jnp.concatenate(parts, axis=1)
            prob[r, j * 256 : (j + 1) * 256] = p
            ctx[r, j * 128 : (j + 1) * 128] = mm(p.astype(BF), keys_of(g, j, 2 * width), NN).astype(BF)
        return 0

    lax.fori_loop(0, units, forward, 0)

    gw0 = gain_ref[...] * iw_ref[0:1, :]
    gw1 = gain_ref[...] * iw_ref[1:2, :]
    slope = (gw1 - gw0) * (1.0 / 16.0)
    slope_mean = jnp.mean(slope)
    base0 = jnp.sum(bias_ref[...] * iw_ref[0:1, :]) + ibias[0]
    base1 = jnp.sum(bias_ref[...] * iw_ref[1:2, :]) + ibias[1]
    part = 192
    tails = part // 16

    def tail(m, _):
        r = pl.ds(pl.multiple_of(m * part, 64), part)
        h = x_ref[r, :].astype(F32) + mm(ctx[r, :], wo_ref[...], NN)
        center = h - jnp.mean(h, axis=-1, keepdims=True)
        spread = jnp.mean(center * center, axis=-1, keepdims=True)
        rstd = lax.rsqrt(spread + 1e-6)
        xhat = center * rstd
        a0 = jnp.sum(xhat * gw0, axis=-1, keepdims=True)
        a1 = jnp.sum(xhat * gw1, axis=-1, keepdims=True)
        l0 = jnp.mean(a0.reshape(tails, 16, 1), axis=1, keepdims=True) + base0
        l1 = jnp.mean(a1.reshape(tails, 16, 1), axis=1, keepdims=True) + base1
        kind = lax.rem(lax.broadcasted_iota(jnp.int32, (tails, 1, 1), 0), 3)
        sign = jnp.where(kind == 0, -1.0, 1.0)
        g1 = sign / (1.0 + jnp.exp(-sign * (l1 - l0)))
        g1 = jnp.broadcast_to(g1, (tails, 16, 1)).reshape(part, 1)
        moved = (a1 - a0) * (1.0 / (16.0 * width))
        g = (rstd * g1) * ((slope - slope_mean) - xhat * moved)
        gh[r, :] = g
        low_g = g.astype(BF)
        ga[r, :] = low_g
        gc[r, :] = mm(low_g, wo_ref[...], NT).astype(BF)
        both = jnp.where(lax.broadcasted_iota(jnp.int32, (tails, 1, 128), 2) == 0, l0, l1)
        logits_ref[pl.ds(m * tails, tails)] = both
        return 0

    lax.fori_loop(0, rows // part, tail, 0)

    def backward(g, _):
        r = pl.ds(pl.multiple_of(g * unit, 32), unit)
        tr = pl.ds(pl.multiple_of(g * 32, 32), 32)
        for j in range(pairs_of_heads):
            c = slice(j * 128, (j + 1) * 128)
            gcj = gc[r, c]
            gp = mm(gcj, keys_of(g, j, 2 * width), NT)
            p = prob[r, j * 256 : (j + 1) * 256]
            gs, pl_low = [], []
            for h in range(2):
                ph = p[:, h * 128 : (h + 1) * 128]
                gph = gp[:, h * 128 : (h + 1) * 128]
                mean = jnp.sum(gph * ph, axis=-1, keepdims=True)
                gs.append((ph * (gph - mean) * scale).astype(BF))
                pl_low.append(ph.astype(BF))
            gq = mm(jnp.concatenate(gs, axis=1), keys_of(g, j, width), NN)
            gk = mm(jnp.concatenate(gs, axis=0), by_head(qkv[r, c]), TN).astype(BF)
            gv = mm(jnp.concatenate(pl_low, axis=0), by_head(gcj), TN).astype(BF)
            gqkv[r, c] = gq.astype(BF)
            gqkv[r, width + j * 128 : width + (j + 1) * 128] = gk[:96]
            gqkv[r, 2 * width + j * 128 : 2 * width + (j + 1) * 128] = gv[:96]
            gt[tr, c] = gk[96:]
            gt[tr, width + j * 128 : width + (j + 1) * 128] = gv[96:]
        return 0

    lax.fori_loop(0, units, backward, 0)

    def to_rows(m, _):
        r = pl.ds(pl.multiple_of(m * part, 64), part)
        g = mm(gqkv[r, :], w_ref[...], NT) + gh[r, :]
        for k in range(part // 48):
            own = pl.ds(pl.multiple_of(m * (part // 3) + k * 16, 16), 16)
            neg = pl.ds(pl.multiple_of(m * (2 * part // 3) + k * 32, 32), 32)
            own_ref[own, :] = g[k * 48 : k * 48 + 16]
            neg_ref[neg, :] = g[k * 48 + 16 : k * 48 + 48].astype(BF)
        return 0

    lax.fori_loop(0, rows // part, to_rows, 0)
    gtext_ref[...] = mm(gt[...], w_ref[:, width:], NT).astype(BF)

    def weight_step(j, _):
        c = pl.ds(pl.multiple_of(j * col, col), col)
        dw_ref[:, c] = mm(x_ref[...], gqkv[:, c], TN)
        return 0

    lax.fori_loop(0, width // col, weight_step, 0)

    def weight_text_step(j, _):
        c = pl.ds(pl.multiple_of(j * col + width, col), col)
        ct = pl.ds(pl.multiple_of(j * col, col), col)
        dw_ref[:, c] = mm(x_ref[...], gqkv[:, c], TN) + mm(t_ref[...], gt[:, ct], TN)
        return 0

    lax.fori_loop(0, 2 * width // col, weight_text_step, 0)

    def out_step(j, _):
        c = pl.ds(pl.multiple_of(j * col, col), col)
        dwo_ref[:, c] = mm(ctx[...], ga[:, c], TN)
        return 0

    lax.fori_loop(0, width // col, out_step, 0)


def attention(images, texts, lens, w, wo, gain, bias, iw, ib):
    rows, width = images.shape
    trows = texts.shape[0]
    vmem = pl.BlockSpec(memory_space=pltpu.VMEM)
    smem = pl.BlockSpec(memory_space=pltpu.SMEM)
    shape = jax.ShapeDtypeStruct
    return pl.pallas_call(
        attention_kernel,
        out_shape=(
            shape((rows // 16, 1, 128), F32),
            shape((trows, width), BF),
            shape((rows // 3, width), F32),
            shape((2 * rows // 3, width), BF),
            shape((width, 3 * width), F32),
            shape((width, width), F32),
        ),
        in_specs=[smem, smem] + [vmem] * 7,
        out_specs=(vmem,) * 6,
        scratch_shapes=[
            pltpu.VMEM((rows, 3 * width), BF),
            pltpu.VMEM((trows, 2 * width), BF),
            pltpu.VMEM((rows, width), BF),
            pltpu.VMEM((rows, width), F32),
            pltpu.VMEM((rows, width), BF),
            pltpu.VMEM((rows, width), BF),
            pltpu.VMEM((rows, 3 * width), BF),
            pltpu.VMEM((trows, 2 * width), BF),
            pltpu.VMEM((rows, 2 * width), F32),
        ],
        compiler_params=pltpu.CompilerParams(vmem_limit_bytes=60 * 1024 * 1024),
        name="pair_attention",
    )(lens, ib, images, texts, w, wo, gain.reshape(1, -1), bias.reshape(1, -1), iw.T)


def on_device(
    text_states, text_len, query_states, neg_owner, neg_slot,
    projection_weight, output_weight, ln_gain, ln_bias, itm_weight, itm_bias,
):
    captions, query_rows, width = query_states.shape
    peers = lax.axis_size("dp")
    requests = captions * CAP
    owner, slot = neg_owner.reshape(-1), neg_slot.reshape(-1)
    ids = jnp.arange(requests)
    rank = jnp.sum(
        ((owner[:, None] == owner[None, :]) & (ids[:, None] > ids[None, :])).astype(jnp.int32), axis=1
    )
    hot = (owner * CAP + rank)[:, None] == jnp.arange(peers * CAP)[None, :]
    wanted = jnp.sum(jnp.where(hot, slot[:, None] + 1, 0), axis=0).reshape(peers, CAP)
    requested = lax.all_to_all(wanted, "dp", split_axis=0, concat_axis=0, tiled=True)
    send = (requested.reshape(-1)[:, None] == jnp.arange(captions)[None, :] + 1).astype(BF)
    flat = query_states.reshape(captions, -1)
    outgoing = jnp.dot(send, flat, preferred_element_type=F32).astype(BF)
    fetched = lax.all_to_all(
        outgoing.reshape(peers, CAP, query_rows, width), "dp", split_axis=0, concat_axis=0, tiled=True
    )
    take = hot.astype(BF)
    negatives = jnp.dot(take, fetched.reshape(peers * CAP, -1), preferred_element_type=F32).astype(BF)
    images = jnp.concatenate(
        [query_states[:, None], negatives.reshape(captions, CAP, query_rows, width)], axis=1
    )
    logits, grad_text, own, back, dw, dwo = attention(
        images.reshape(-1, width), text_states.reshape(-1, width), text_len,
        projection_weight, output_weight, ln_gain, ln_bias, itm_weight, itm_bias,
    )
    outgoing_grads = jnp.dot(take.T, back.reshape(requests, -1), preferred_element_type=F32).astype(BF)
    returned = lax.all_to_all(
        outgoing_grads.reshape(peers, CAP, query_rows, width), "dp", split_axis=0, concat_axis=0, tiled=True
    )
    sum_qkv, sum_out = lax.psum((dw, dwo), "dp")
    received = jnp.dot(send.T, returned.reshape(peers * CAP, -1), preferred_element_type=F32)
    grad_query = (own.reshape(captions, -1) + received).astype(BF).reshape(query_states.shape)
    total = captions * peers
    return (
        logits[:, 0, :2].reshape(captions, 3, 2),
        grad_text.reshape(text_states.shape),
        grad_query,
        sum_qkv / total,
        sum_out / total,
    )


def solution(mesh):
    rows = P("dp", None, None)
    placed = (rows, P("dp"), rows, P("dp", None), P("dp", None)) + (P(),) * 6
    return jax.shard_map(
        on_device, mesh=mesh, in_specs=placed, out_specs=(rows, rows, rows, P(), P()), check_vma=False
    )
```

time: 800 us -> 448 us (0.56)
  matrix products: 187 us -> 5.96 us
  local copies, waits for them, and re-layouts: 157 us -> 28.6 us
  other arithmetic: 122 us -> 12.5 us
  Pallas kernels: 0 us -> 61.8 us
  waiting for transfers between devices: 289 us -> 301 us
    dot_general x21 -> x4, matrix products: 187 us -> 5.96 us  [the longest x1 1.89 us: on_device(): jnp.dot(take.T, back.reshape(requests, -1), preferred_element_type=F32)]
    sub x2 -> x0, other arithmetic: 97.7 us -> none  [the longest x1 97.7 us: pair_work(): shifted = jnp.exp(scores - jnp.max(scores, axis=-1, keepdims=True))]
    reshape x11 -> x5, local copies, waits for them, and re-layouts: 72.3 us -> 3.1 us  [the longest x1 1.69 us: on_device(): back.reshape(requests, -1)]
    pallas_call x0 -> x1, Pallas kernels: none -> 61.8 us  [attention(): pl.pallas_call(attention_kernel, out_shape=(shape((rows // 16, 1, 128), F...]
    transpose x3 -> x0, local copies, waits for them, and re-layouts: 32.9 us -> none  [matrix_product(): jnp.einsum(einsum_form, left_side, right_side, preferred_element_type=jnp...]
    slice x8 -> x1, local copies, waits for them, and re-layouts: 16.6 us -> 0.07 us  [on_device(): logits[:, 0, :2].reshape(captions, 3, 2)]
    unnamed x92 -> x19, local copies, waits for them, and re-layouts: 31 us -> 23.8 us
where the time goes in v1:
time: 448 us; the launch traced here: 447 us
  waiting for transfers between devices  301 us (67%)
  Pallas kernels  61.8 us (14%)
  local copies, waits for them, and re-layouts  28.6 us (6%)
  starting transfers between devices  23 us (5%)
  between operations  14.2 us (3%)
  other arithmetic  12.5 us (3%)
  matrix products  5.96 us (1%)
    psum x1, waiting for transfers between devices, on_device(): sum_qkv, sum_out = lax.psum((dw, dwo), 'dp')  218 us
    all_to_all x1, waiting for transfers between devices, on_device(): lax.all_to_all(outgoing.reshape(peers, CAP, query_rows, width), 'dp', spl...  74.2 us
    pallas_call x1, Pallas kernels, attention(): pl.pallas_call(attention_kernel, out_shape=(shape((rows // 16, 1, 128), F...  61.8 us
    unnamed x19, local copies, waits for them, and re-layouts  23.8 us
    all_to_all x1, starting transfers between devices, on_device(): lax.all_to_all(wanted, 'dp', split_axis=0, concat_axis=0, tiled=True)  11.5 us
  transfers between devices with their start and end apart: 4, of which 3 were waited for; matrix products, arithmetic and copies ran while one was open for 3% of the time, Pallas kernels for 0%

profile of v1, /device:TPU:1, one launch (start us, length us, event | category | flops | bytes accessed | tf_op | source)
XLA Modules:
  0.0 447.0 jit_solution(10587766918576765598)
XLA Ops:
  7.2 0.7 broadcast_add_fusion
  8.0 0.8 copy.32
  8.9 0.2 convert_reduce_fusion
  9.2 0.8 all_to_all.12
  9.9 11.5 %all-to-all-start = ((s32[128,1,2]{2,1,0:T(1,128)}), s32[128,1,2]{2,1,0:T(1,128)S(1)}, u32[]{:S(2)}, u32[]{:S(2)}) async-start(s32[128,1,2]{2,1,0:T(1,128)} %bitcast.2), calls=%async_computation | async-start | bytes 131072 | tf_op jit(solution)/shard_map/all_to_all | solution.py:234
  21.5 1.1 copy.38
  22.6 8.4 %all-to-all-done = s32[128,1,2]{2,1,0:T(1,128)S(1)} async-done(((s32[128,1,2]{2,1,0:T(1,128)}), s32[128,1,2]{2,1,0:T(1,128)S(1)}, u32[]{:S(2)}, u32[]{:S(2)}) %all-to-all-start) | async-done | bytes 1056 | tf_op jit(solution)/shard_map/all_to_all | solution.py:234
  31.0 0.5 broadcast.26
  31.5 0.8 reduce.3
  32.4 1.8 convolution_convert_fusion
  34.3 4.6 %copy.39 = bf16[32,8,16,768]{3,2,1,0:T(8,128)(2,1)} copy(bf16[32,8,16,768]{3,1,2,0:T(8,128)(2,1)S(1)} %bitcast.37) | data formatting | bytes 12582912
  38.9 5.4 %all-to-all-start.1 = ((bf16[128,2,16,768]{3,2,1,0:T(8,128)(2,1)}), bf16[128,2,16,768]{3,2,1,0:T(8,128)(2,1)}, u32[]{:S(2)}, u32[]{:S(2)}) async-start(bf16[128,2,16,768]{3,2,1,0:T(8,128)(2,1)} %bitcast.35), calls=%async_computation.1 | async-start | bytes 12582912 | tf_op jit(solution)/shard_map/all_to_all | solution.py:238
  44.3 0.6 reshape.92.gain_ref
  44.9 0.6 reshape.93.bias_ref
  45.5 74.2 %all-to-all-done.1 = bf16[128,2,16,768]{3,2,1,0:T(8,128)(2,1)} async-done(((bf16[128,2,16,768]{3,2,1,0:T(8,128)(2,1)}), bf16[128,2,16,768]{3,2,1,0:T(8,128)(2,1)}, u32[]{:S(2)}, u32[]{:S(2)}) %all-to-all-start.1) | async-done | bytes 6291488 | tf_op jit(solution)/shard_map/all_to_all | solution.py:238
  119.7 5.6 %copy.40 = bf16[32,8,16,768]{3,1,2,0:T(8,128)(2,1)S(1)} copy(bf16[32,8,16,768]{3,2,1,0:T(8,128)(2,1)} %bitcast.14) | data formatting | bytes 12582912
  125.2 1.2 convolution_convert_fusion.2
  126.4 0.2 copy.41
  126.6 1.1 pad_maximum_fusion
  127.7 61.8 %pair_attention.1 = (f32[48,1,128]{2,1,0:T(1,128)}, bf16[256,768]{1,0:T(8,128)(2,1)}, f32[256,768]{1,0:T(8,128)}, bf16[512,768]{1,0:T(8,128)(2,1)}, f32[768,2304]{1,0:T(8,128)}, /*index=5*/f32[768,768]{1,0:T(8,128)}) custom-call(s32[16]{0:T(128)} %lens.1, f32[2]{0:T(128)} %ibias.1, bf16[768,768]{1,0:T(8,128)(2,1)} %bitcast.40, bf16[256,768]{1,0:T(8,128)(2,1)} %bitcast.47, ...), custom_call_target="tpu_custom_call" | custom-call | tf_op jit(solution)/shard_map/pair_attention/pallas_call | solution.py:192
  189.5 1.7 reshape.96
  191.2 1.9 convolution_convert_fusion.1
  193.1 4.5 %copy.42 = bf16[32,8,16,768]{3,2,1,0:T(8,128)(2,1)} copy(bf16[32,8,16,768]{3,1,2,0:T(8,128)(2,1)S(1)} %bitcast.38) | data formatting | bytes 12582912
  197.6 6.1 %all-to-all-start.2 = ((bf16[128,2,16,768]{3,2,1,0:T(8,128)(2,1)}), bf16[128,2,16,768]{3,2,1,0:T(8,128)(2,1)}, u32[]{:S(2)}, u32[]{:S(2)}) async-start(bf16[128,2,16,768]{3,2,1,0:T(8,128)(2,1)} %bitcast.34), calls=%async_computation.2 | async-start | bytes 12582912 | tf_op jit(solution)/shard_map/all_to_all | solution.py:251
  203.7 0.7 all-reduce.3.cloned.1.call-update
  204.6 0.7 copy.37
  205.4 217.7 %all-reduce.3.cloned.1.call-done = (f32[768,2304]{1,0:T(8,128)}, f32[768,768]{1,0:T(8,128)}) async-done(((f32[768,2304]{1,0:T(8,128)}, f32[768,768]{1,0:T(8,128)}), (f32[768,2304]{1,0:T(8,128)}, f32[768,768]{1,0:T(8,128)})) %all-reduce.3.cloned.1.call-update) | async-done | bytes 9437200 | tf_op jit(solution)/shard_map/psum | solution.py:254
  423.1 3.2 broadcast_multiply_fusion.1
  426.3 6.4 %broadcast_multiply_fusion = f32[768,2304]{1,0:T(8,128)} fusion(f32[768,2304]{1,0:T(8,128)} %get-tuple-element.37), kind=kLoop, calls=%fused_computation.5 | loop fusion | flops 1769472 | bytes 14155776 | tf_op jit(solution)/shard_map/div | solution.py:262
  432.8 5.6 %copy.43 = bf16[32,8,16,768]{3,1,2,0:T(8,128)(2,1)S(1)} copy(bf16[32,8,16,768]{3,2,1,0:T(8,128)(2,1)} %bitcast.24) | data formatting | bytes 12582912
  438.3 1.0 fusion
  439.4 0.8 copy.44
  (22 shorter events, 0.9 us)
Async XLA Ops:
  9.9 21.0 %all-to-all-start = ((s32[128,1,2]{2,1,0:T(1,128)}), s32[128,1,2]{2,1,0:T(1,128)S(1)}, u32[]{:S(2)}, u32[]{:S(2)}) async-start(s32[128,1,2]{2,1,0:T(1,128)} %bitcast.2), calls=%async_computation | async-start | bytes 131072 | tf_op jit(solution)/shard_map/all_to_all | solution.py:234
  38.9 5.5 %copy-start.3 = (f32[768]{0:T(1024)S(1)}, f32[768]{0:T(1024)}, u32[]{:S(2)}) copy-start(f32[768]{0:T(1024)} %param.18) | copy-start | bytes 9220
  38.9 6.0 %copy-start.4 = (f32[768]{0:T(1024)S(1)}, f32[768]{0:T(1024)}, u32[]{:S(2)}) copy-start(f32[768]{0:T(1024)} %param.19) | copy-start | bytes 9220
  38.9 80.8 %all-to-all-start.1 = ((bf16[128,2,16,768]{3,2,1,0:T(8,128)(2,1)}), bf16[128,2,16,768]{3,2,1,0:T(8,128)(2,1)}, u32[]{:S(2)}, u32[]{:S(2)}) async-start(bf16[128,2,16,768]{3,2,1,0:T(8,128)(2,1)} %bitcast.35), calls=%async_computation.1 | async-start | bytes 12582912 | tf_op jit(solution)/shard_map/all_to_all | solution.py:238
  125.2 1.4 copy-start
  197.6 235.2 %all-to-all-start.2 = ((bf16[128,2,16,768]{3,2,1,0:T(8,128)(2,1)}), bf16[128,2,16,768]{3,2,1,0:T(8,128)(2,1)}, u32[]{:S(2)}, u32[]{:S(2)}) async-start(bf16[128,2,16,768]{3,2,1,0:T(8,128)(2,1)} %bitcast.34), calls=%async_computation.2 | async-start | bytes 12582912 | tf_op jit(solution)/shard_map/all_to_all | solution.py:251
  203.7 0.8 copy-start.2
  203.7 1.6 copy-start.1
  203.7 219.4 %all-reduce.3.cloned.1.call-start = ((), (), s32[]{:S(2)}) async-start(), calls=%async_computation.3 | async-start | bytes 18874368 | tf_op jit(solution)/shard_map/psum | solution.py:254
Sparse Core Ops, SparseCore 0:
  210.1 212.9 all-reduce.2

commit v2 on v1

--- a/solution.py
+++ b/solution.py
@@ -6,7 +6,6 @@
 from jax.experimental.pallas import tpu as pltpu
 from jax.sharding import PartitionSpec as P
 
-CAP = 2
 F32 = jnp.float32
 BF = jnp.bfloat16
 NN = (((1,), (0,)), ((), ()))
@@ -20,7 +19,7 @@
 
 def attention_kernel(
     lens, ibias, x_ref, t_ref, w_ref, wo_ref, gain_ref, bias_ref, iw_ref,
-    logits_ref, gtext_ref, own_ref, neg_ref, dw_ref, dwo_ref,
+    logits_ref, gtext_ref, own_ref, neg_ref, dw_ref,
     qkv, tkv, ctx, gh, ga, gc, gqkv, gt, prob,
 ):
     rows, width = x_ref.shape
@@ -162,7 +161,7 @@
 
     def weight_step(j, _):
         c = pl.ds(pl.multiple_of(j * col, col), col)
-        dw_ref[:, c] = mm(x_ref[...], gqkv[:, c], TN)
+        dw_ref[j] = mm(x_ref[...], gqkv[:, c], TN).astype(BF)
         return 0
 
     lax.fori_loop(0, width // col, weight_step, 0)
@@ -170,14 +169,15 @@
     def weight_text_step(j, _):
         c = pl.ds(pl.multiple_of(j * col + width, col), col)
         ct = pl.ds(pl.multiple_of(j * col, col), col)
-        dw_ref[:, c] = mm(x_ref[...], gqkv[:, c], TN) + mm(t_ref[...], gt[:, ct], TN)
+        total = mm(x_ref[...], gqkv[:, c], TN) + mm(t_ref[...], gt[:, ct], TN)
+        dw_ref[j + width // col] = total.astype(BF)
         return 0
 
     lax.fori_loop(0, 2 * width // col, weight_text_step, 0)
 
     def out_step(j, _):
         c = pl.ds(pl.multiple_of(j * col, col), col)
-        dwo_ref[:, c] = mm(ctx[...], ga[:, c], TN)
+        dw_ref[j + 3 * width // col] = mm(ctx[...], ga[:, c], TN).astype(BF)
         return 0
 
     lax.fori_loop(0, width // col, out_step, 0)
@@ -196,11 +196,10 @@
             shape((trows, width), BF),
             shape((rows // 3, width), F32),
             shape((2 * rows // 3, width), BF),
-            shape((width, 3 * width), F32),
-            shape((width, width), F32),
+            shape((4 * width // 256, width, 256), BF),
         ),
         in_specs=[smem, smem] + [vmem] * 7,
-        out_specs=(vmem,) * 6,
+        out_specs=(vmem,) * 5,
         scratch_shapes=[
             pltpu.VMEM((rows, 3 * width), BF),
             pltpu.VMEM((trows, 2 * width), BF),
@@ -217,50 +216,433 @@
     )(lens, ib, images, texts, w, wo, gain.reshape(1, -1), bias.reshape(1, -1), iw.T)
 
 
+HOLDERS = 48
+PIECE = 256
+MESH = pl.DeviceIdType.MESH
+
+
+def place():
+    me = lax.axis_index("dp")
+    return me, me // 32, (me // 8) % 4, (me // 2) % 4, me % 2
+
+
+def device_at(z, y, x, core):
+    return ((z * 4 + y) * 4 + x) * 2 + core
+
+
+def holder(piece):
+    line, k = piece // 3, piece % 3
+    z, y = line // 4, line % 4
+    return device_at(z, y, (k + 8 - y - z) % 4, piece % 2)
+
+
+def held_piece():
+    me, z, y, x, core = place()
+    k = (x + y + z) % 4
+    piece = (z * 4 + y) * 3 + k
+    return piece, (k < 3) & (core == piece % 2)
+
+
+def one_hot(mask):
+    return jnp.where(mask, 1.0, 0.0).astype(BF)
+
+
+def swap_rows(outer, inner):
+    n = outer * inner
+    to = lax.broadcasted_iota(jnp.int32, (n, n), 0)
+    source = lax.broadcasted_iota(jnp.int32, (n, n), 1)
+    return one_hot(source == lax.rem(to, outer) * inner + lax.div(to, outer))
+
+
+def fetch_kernel(q_ref, need_ref, out_ref, table_ref, pieces, held, picked, arrived,
+                 send_sem, held_sem, index_send, index_sem, pick_send, pick_sem):
+    me = lax.axis_index("dp")
+    mine, holding = held_piece()
+    peers = held.shape[0]
+    slots = arrived.shape[1]
+    images = pieces.shape[1]
+    swapped = mm(swap_rows(images, 16), q_ref[...], NN).astype(BF)
+    for r in range(16):
+        for k in range(3):
+            pieces[r * 3 + k] = swapped[r * images : (r + 1) * images, k * PIECE : (k + 1) * PIECE]
+
+    def spread(i, _):
+        piece = (i + me) % HOLDERS
+        target = holder(piece)
+
+        @pl.when(target != me)
+        def _():
+            pltpu.make_async_remote_copy(
+                src_ref=need_ref, dst_ref=table_ref.at[me], send_sem=index_send, recv_sem=index_sem,
+                device_id=(target,), device_id_type=MESH).start()
+            pltpu.make_async_remote_copy(
+                src_ref=pieces.at[piece], dst_ref=held.at[me], send_sem=send_sem, recv_sem=held_sem,
+                device_id=(target,), device_id_type=MESH).start()
+
+        @pl.when(target == me)
+        def _():
+            pltpu.make_async_copy(need_ref, table_ref.at[me], index_sem).start()
+            pltpu.make_async_copy(pieces.at[piece], held.at[me], held_sem).start()
+
+        return 0
+
+    lax.fori_loop(0, HOLDERS, spread, 0)
+
+    @pl.when(holding)
+    def _():
+        pltpu.make_async_copy(table_ref, table_ref, index_sem).wait()
+        pltpu.make_async_copy(held, held, held_sem).wait()
+        lanes = lax.broadcasted_iota(jnp.int32, (slots, 128), 1)
+        lines = lax.broadcasted_iota(jnp.int32, (slots, 128), 0)
+        ids = lax.broadcasted_iota(jnp.int32, (1, 2048), 1).astype(F32) + 1.0
+        values = held.reshape(2048, PIECE)
+
+        def pick(g, _):
+            columns = []
+            for b in range(8):
+                row = table_ref[g * 8 + b].astype(F32)
+                eye = lanes == lines + 32 * (b % 4)
+                columns.append(jnp.sum(jnp.where(eye, row, 0.0), axis=-1, keepdims=True))
+            hot = one_hot(jnp.concatenate(columns, axis=0) == ids)
+            chosen = mm(hot, values[...], NN).astype(BF)
+            for b in range(8):
+                target = g * 8 + b
+                picked[target] = chosen[b * slots : (b + 1) * slots]
+
+                @pl.when(target != me)
+                def _():
+                    pltpu.make_async_remote_copy(
+                        src_ref=picked.at[target], dst_ref=arrived.at[mine], send_sem=pick_send,
+                        recv_sem=pick_sem, device_id=(target,), device_id_type=MESH).start()
+
+                @pl.when(target == me)
+                def _():
+                    pltpu.make_async_copy(picked.at[target], arrived.at[mine], pick_sem).start()
+
+            return 0
+
+        lax.fori_loop(0, peers // 8, pick, 0)
+
+    swap = swap_rows(16, slots)
+    pltpu.make_async_copy(arrived, arrived, pick_sem).wait()
+    for k in range(3):
+        c = slice(k * PIECE, (k + 1) * PIECE)
+        stacked = jnp.concatenate([arrived[r * 3 + k] for r in range(16)], axis=0)
+        block = mm(swap, stacked, NN).astype(BF)
+        for i in range(images):
+            out_ref[i * 48 : i * 48 + 16, c] = q_ref[i * 16 : (i + 1) * 16, c]
+            out_ref[i * 48 + 16 : i * 48 + 48, c] = block[i * 32 : (i + 1) * 32]
+
+    @pl.when(holding)
+    def _():
+        pltpu.make_async_copy(pieces.at[0 : HOLDERS - 1], pieces.at[0 : HOLDERS - 1], send_sem).wait()
+        pltpu.make_async_copy(table_ref.at[0 : HOLDERS - 1], table_ref.at[0 : HOLDERS - 1], index_send).wait()
+        pltpu.make_async_copy(picked.at[0 : peers - 1], picked.at[0 : peers - 1], pick_send).wait()
+
+    @pl.when(jnp.logical_not(holding))
+    def _():
+        pltpu.make_async_copy(pieces, pieces, send_sem).wait()
+        pltpu.make_async_copy(table_ref.at[0:HOLDERS], table_ref.at[0:HOLDERS], index_send).wait()
+
+
+def fetch(queries, need, peers):
+    rows, width = queries.shape
+    images = rows // 16
+    vmem = pl.BlockSpec(memory_space=pltpu.VMEM)
+    return pl.pallas_call(
+        fetch_kernel,
+        out_shape=(
+            jax.ShapeDtypeStruct((3 * rows, width), BF),
+            jax.ShapeDtypeStruct((peers, 1, 128), jnp.int32),
+        ),
+        in_specs=[vmem, vmem],
+        out_specs=(vmem, vmem),
+        scratch_shapes=[
+            pltpu.VMEM((HOLDERS, images, PIECE), BF),
+            pltpu.VMEM((peers, images, PIECE), BF),
+            pltpu.VMEM((peers, 2 * images, PIECE), BF),
+            pltpu.VMEM((HOLDERS, 2 * images, PIECE), BF),
+        ]
+        + [pltpu.SemaphoreType.DMA] * 6,
+        compiler_params=pltpu.CompilerParams(vmem_limit_bytes=48 * 1024 * 1024, has_side_effects=True),
+        name="fetch_negatives",
+    )(queries, need)
+
+
+def reduce_kernel(
+    g_ref, back_ref, own_ref, table_ref, sum_ref, query_ref,
+    half_in, half, in1, sum1, in2, sum2, in3, pieces, held, totals, arrived,
+    s_send, s_recv, a_send, a_recv, piece_send, held_sem, total_send, total_sem,
+):
+    me, z, y, x, core = place()
+    mine, holding = held_piece()
+    spots = (x, y, z)
+    peers, slots = held.shape[0], held.shape[1]
+    images = totals.shape[1]
+    thirds = range(3)
+
+    def along(axis, step):
+        at = [x, y, z]
+        at[axis] = (at[axis] + step) % 4
+        return device_at(at[2], at[1], at[0], core)
+
+    def axis_of(t, stage):
+        return (t + stage) % 3
+
+    twin = me + 1 - 2 * core
+    mine_rows = pl.ds(pl.multiple_of(core * 384, 128), 384)
+    twin_rows = pl.ds(pl.multiple_of(384 - core * 384, 128), 384)
+
+    def remote(source, target, send, recv, device):
+        return pltpu.make_async_remote_copy(
+            src_ref=source, dst_ref=target, send_sem=send, recv_sem=recv,
+            device_id=(device,), device_id_type=MESH)
+
+    sends = []
+
+    def start(copy):
+        copy.start()
+        sends.append(copy)
+
+    zero = [
+        remote(g_ref.at[pl.ds(4 * t, 4), twin_rows], half_in.at[pl.ds(4 * t, 4)],
+               s_send.at[t, 0], s_recv.at[t, 0], twin)
+        for t in thirds
+    ]
+    for copy in zero:
+        start(copy)
+
+    swapped = mm(swap_rows(slots, 16), back_ref[...], NN).astype(BF)
+    for r in range(16):
+        for k in range(3):
+            pieces[r * 3 + k] = swapped[r * slots : (r + 1) * slots, k * PIECE : (k + 1) * PIECE]
+
+    def spread(i, _):
+        piece = (i + me) % HOLDERS
+        target = holder(piece)
+
+        @pl.when(target != me)
+        def _():
+            remote(pieces.at[piece], held.at[me], piece_send, held_sem, target).start()
+
+        @pl.when(target == me)
+        def _():
+            pltpu.make_async_copy(pieces.at[piece], held.at[me], held_sem).start()
+
+        return 0
+
+    lax.fori_loop(0, HOLDERS, spread, 0)
+
+    one = {}
+    for t in thirds:
+        zero[t].wait_recv()
+        axis = axis_of(t, 0)
+
+        def add_half(k, _, t=t):
+            own = g_ref[4 * t + k, mine_rows, :].astype(F32)
+            half[4 * t + k] = (own + half_in[4 * t + k].astype(F32)).astype(BF)
+            return 0
+
+        lax.fori_loop(0, 4, add_half, 0)
+        for d in (1, 2, 3):
+            to = (spots[axis] + d) % 4
+            one[t, d] = remote(half.at[4 * t + to], in1.at[t, d - 1],
+                               s_send.at[t, d], s_recv.at[t, d], along(axis, d))
+            start(one[t, d])
+
+    @pl.when(holding)
+    def _():
+        pltpu.make_async_copy(held, held, held_sem).wait()
+        values = held.reshape(peers * slots, PIECE)
+        ids = lax.broadcasted_iota(jnp.int32, (256, 128), 0).astype(F32) + 1.0
+        rows = [
+            table_ref[4 * b].astype(F32) + table_ref[4 * b + 1].astype(F32)
+            + table_ref[4 * b + 2].astype(F32) + table_ref[4 * b + 3].astype(F32)
+            for b in range(peers // 4)
+        ]
+
+        def add_up(g, _):
+            shift = (g * 256).astype(F32)
+            hot = jnp.concatenate([one_hot(ids == row - shift) for row in rows], axis=1)
+            total = mm(hot, values[...], NN).astype(BF)
+            for b in range(16):
+                target = g * 16 + b
+                totals[target] = total[b * images : (b + 1) * images]
+
+                @pl.when(target != me)
+                def _():
+                    remote(totals.at[target], arrived.at[mine], total_send, total_sem, target).start()
+
+                @pl.when(target == me)
+                def _():
+                    pltpu.make_async_copy(totals.at[target], arrived.at[mine], total_sem).start()
+
+            return 0
+
+        lax.fori_loop(0, peers // 16, add_up, 0)
+
+    two = {}
+    for t in thirds:
+        axis, after = axis_of(t, 0), axis_of(t, 1)
+        for d in (1, 2, 3):
+            one[t, d].wait_recv()
+        total = half[4 * t + spots[axis]].astype(F32)
+        for d in range(3):
+            total += in1[t, d].astype(F32)
+        sum1[t] = total.astype(BF)
+        for d in (1, 2, 3):
+            to = (spots[after] + d) % 4
+            two[t, d] = remote(sum1.at[t, pl.ds(pl.multiple_of(to * 96, 32), 96)], in2.at[t, d - 1],
+                               s_send.at[t, 3 + d], s_recv.at[t, 3 + d], along(after, d))
+            start(two[t, d])
+
+    def corner(ref, first, spot):
+        rows = pl.ds(pl.multiple_of(first + (spot // 2) * 48, 16), 48)
+        return ref.at[rows, pl.ds(pl.multiple_of((spot % 2) * 128, 128), 128)]
+
+    three = {}
+    for t in thirds:
+        axis, after = axis_of(t, 1), axis_of(t, 2)
+        for d in (1, 2, 3):
+            two[t, d].wait_recv()
+        total = sum1[t, pl.ds(pl.multiple_of(spots[axis] * 96, 32), 96), :].astype(F32)
+        for d in range(3):
+            total += in2[t, d].astype(F32)
+        sum2[t] = total.astype(BF)
+        for d in (1, 2, 3):
+            to = (spots[after] + d) % 4
+            three[t, d] = remote(corner(sum2.at[t], 0, to), in3.at[t, d - 1],
+                                 s_send.at[t, 6 + d], s_recv.at[t, 6 + d], along(after, d))
+            start(three[t, d])
+
+    last = {}
+    for t in thirds:
+        axis = axis_of(t, 2)
+        for d in (1, 2, 3):
+            three[t, d].wait_recv()
+        total = corner(sum2.at[t], 0, spots[axis])[...].astype(F32)
+        for d in range(3):
+            total += in3[t, d].astype(F32)
+        block = sum_ref.at[4 * t + spots[axis_of(t, 0)]]
+        first = core * 384 + spots[axis_of(t, 1)] * 96
+        piece = corner(block, first, spots[axis])
+        piece[...] = total.astype(BF)
+        for d in (1, 2, 3):
+            last[t, d] = remote(piece, piece, a_send.at[t, d], a_recv.at[t, d], along(axis, d))
+            start(last[t, d])
+
+    def came(t, stage, ref, d):
+        return pltpu.make_async_copy(ref, ref, a_recv.at[t, stage * 3 + d])
+
+    for t in thirds:
+        axis = axis_of(t, 1)
+        block = sum_ref.at[4 * t + spots[axis_of(t, 0)]]
+        first = core * 384 + spots[axis] * 96
+        for d in (1, 2, 3):
+            came(t, 0, corner(block, first, (spots[axis_of(t, 2)] + 4 - d) % 4), d).wait()
+        piece = block.at[pl.ds(pl.multiple_of(first, 32), 96)]
+        for d in (1, 2, 3):
+            start(remote(piece, piece, a_send.at[t, 3 + d], a_recv.at[t, 3 + d], along(axis, d)))
+
+    for t in thirds:
+        axis = axis_of(t, 0)
+        block = sum_ref.at[4 * t + spots[axis]]
+        for d in (1, 2, 3):
+            spot = (spots[axis_of(t, 1)] + 4 - d) % 4
+            came(t, 1, block.at[pl.ds(pl.multiple_of(core * 384 + spot * 96, 32), 96)], d).wait()
+        piece = block.at[mine_rows]
+        for d in (1, 2, 3):
+            start(remote(piece, piece, a_send.at[t, 6 + d], a_recv.at[t, 6 + d], along(axis, d)))
+
+    for t in thirds:
+        axis = axis_of(t, 0)
+        for d in (1, 2, 3):
+            spot = (spots[axis] + 4 - d) % 4
+            came(t, 2, sum_ref.at[4 * t + spot, mine_rows], d).wait()
+        piece = sum_ref.at[pl.ds(4 * t, 4), mine_rows]
+        start(remote(piece, piece, a_send.at[t, 0], a_recv.at[t, 0], twin))
+
+    pltpu.make_async_copy(arrived, arrived, total_sem).wait()
+    swap = swap_rows(16, images)
+    for k in range(3):
+        c = slice(k * PIECE, (k + 1) * PIECE)
+        stacked = jnp.concatenate([arrived[r * 3 + k] for r in range(16)], axis=0)
+        query_ref[:, c] = (own_ref[:, c] + mm(swap, stacked, NN)).astype(BF)
+
+    for t in thirds:
+        other = sum_ref.at[pl.ds(4 * t, 4), twin_rows]
+        pltpu.make_async_copy(other, other, a_recv.at[t, 0]).wait()
+    for copy in sends:
+        copy.wait_send()
+
+    @pl.when(holding)
+    def _():
+        pltpu.make_async_copy(pieces.at[0 : HOLDERS - 1], pieces.at[0 : HOLDERS - 1], piece_send).wait()
+        pltpu.make_async_copy(totals.at[0 : peers - 1], totals.at[0 : peers - 1], total_send).wait()
+
+    @pl.when(jnp.logical_not(holding))
+    def _():
+        pltpu.make_async_copy(pieces, pieces, piece_send).wait()
+
+
+def reduce(grads, back, own, table):
+    peers = table.shape[0]
+    rows, width = own.shape
+    images = rows // 16
+    vmem = pl.BlockSpec(memory_space=pltpu.VMEM)
+    dma = pltpu.SemaphoreType.DMA
+    return pl.pallas_call(
+        reduce_kernel,
+        out_shape=(
+            jax.ShapeDtypeStruct(grads.shape, BF),
+            jax.ShapeDtypeStruct(own.shape, BF),
+        ),
+        in_specs=[vmem] * 4,
+        out_specs=(vmem, vmem),
+        scratch_shapes=[
+            pltpu.VMEM((12, 384, 256), BF),
+            pltpu.VMEM((12, 384, 256), BF),
+            pltpu.VMEM((3, 3, 384, 256), BF),
+            pltpu.VMEM((3, 384, 256), BF),
+            pltpu.VMEM((3, 3, 96, 256), BF),
+            pltpu.VMEM((3, 96, 256), BF),
+            pltpu.VMEM((3, 3, 48, 128), BF),
+            pltpu.VMEM((HOLDERS, 2 * images, PIECE), BF),
+            pltpu.VMEM((peers, 2 * images, PIECE), BF),
+            pltpu.VMEM((peers, images, PIECE), BF),
+            pltpu.VMEM((HOLDERS, images, PIECE), BF),
+            dma((3, 10)), dma((3, 10)), dma((3, 10)), dma((3, 10)),
+            dma, dma, dma, dma,
+        ],
+        compiler_params=pltpu.CompilerParams(vmem_limit_bytes=56 * 1024 * 1024, has_side_effects=True),
+        name="sum_gradients",
+    )(grads, back, own, table)
+
+
 def on_device(
     text_states, text_len, query_states, neg_owner, neg_slot,
     projection_weight, output_weight, ln_gain, ln_bias, itm_weight, itm_bias,
 ):
     captions, query_rows, width = query_states.shape
     peers = lax.axis_size("dp")
-    requests = captions * CAP
-    owner, slot = neg_owner.reshape(-1), neg_slot.reshape(-1)
-    ids = jnp.arange(requests)
-    rank = jnp.sum(
-        ((owner[:, None] == owner[None, :]) & (ids[:, None] > ids[None, :])).astype(jnp.int32), axis=1
-    )
-    hot = (owner * CAP + rank)[:, None] == jnp.arange(peers * CAP)[None, :]
-    wanted = jnp.sum(jnp.where(hot, slot[:, None] + 1, 0), axis=0).reshape(peers, CAP)
-    requested = lax.all_to_all(wanted, "dp", split_axis=0, concat_axis=0, tiled=True)
-    send = (requested.reshape(-1)[:, None] == jnp.arange(captions)[None, :] + 1).astype(BF)
-    flat = query_states.reshape(captions, -1)
-    outgoing = jnp.dot(send, flat, preferred_element_type=F32).astype(BF)
-    fetched = lax.all_to_all(
-        outgoing.reshape(peers, CAP, query_rows, width), "dp", split_axis=0, concat_axis=0, tiled=True
-    )
-    take = hot.astype(BF)
-    negatives = jnp.dot(take, fetched.reshape(peers * CAP, -1), preferred_element_type=F32).astype(BF)
-    images = jnp.concatenate(
-        [query_states[:, None], negatives.reshape(captions, CAP, query_rows, width)], axis=1
-    )
-    logits, grad_text, own, back, dw, dwo = attention(
-        images.reshape(-1, width), text_states.reshape(-1, width), text_len,
+    me = lax.axis_index("dp")
+    wanted = (captions * neg_owner + neg_slot + 1).reshape(1, 2 * captions)
+    group = jnp.arange(4)[:, None] == me % 4
+    need = jnp.where(group, wanted, 0).reshape(1, 128)
+    images, table = fetch(query_states.reshape(-1, width), need, peers)
+    logits, grad_text, own, back, grads = attention(
+        images, text_states.reshape(-1, width), text_len,
         projection_weight, output_weight, ln_gain, ln_bias, itm_weight, itm_bias,
     )
-    outgoing_grads = jnp.dot(take.T, back.reshape(requests, -1), preferred_element_type=F32).astype(BF)
-    returned = lax.all_to_all(
-        outgoing_grads.reshape(peers, CAP, query_rows, width), "dp", split_axis=0, concat_axis=0, tiled=True
-    )
-    sum_qkv, sum_out = lax.psum((dw, dwo), "dp")
-    received = jnp.dot(send.T, returned.reshape(peers * CAP, -1), preferred_element_type=F32)
-    grad_query = (own.reshape(captions, -1) + received).astype(BF).reshape(query_states.shape)
-    total = captions * peers
+    sums, grad_query = reduce(grads, back, own, table)
+    share = 1.0 / (captions * peers)
+    sums = sums.transpose(1, 0, 2).reshape(width, 4 * width).astype(F32) * share
     return (
         logits[:, 0, :2].reshape(captions, 3, 2),
         grad_text.reshape(text_states.shape),
-        grad_query,
-        sum_qkv / total,
-        sum_out / total,
+        grad_query.reshape(query_states.shape),
+        sums[:, : 3 * width],
+        sums[:, 3 * width :],
     )
 
 

time: 448 us -> 223 us (0.50)
  waiting for transfers between devices: 301 us -> 0 us
  Pallas kernels: 61.8 us -> 178 us
  starting transfers between devices: 23 us -> 0 us
  between operations: 14.2 us -> 0.69 us
  local copies, waits for them, and re-layouts: 28.6 us -> 35.5 us
  matrix products: 5.96 us -> 0 us
  other arithmetic: 12.5 us -> 7.67 us
    psum x1 -> x0, waiting for transfers between devices: 218 us -> none  [on_device(): sum_qkv, sum_out = lax.psum((dw, dwo), 'dp')]
    pallas_call x0 -> x2, Pallas kernels: none -> 118 us  [the longest x1 82.3 us: reduce(): pl.pallas_call(reduce_kernel, out_shape=(jax.ShapeDtypeStruct(grads.shape...]
    all_to_all x3 -> x0, waiting for transfers between devices: 82.6 us -> none  [the longest x1 74.2 us: on_device(): lax.all_to_all(outgoing.reshape(peers, CAP, query_rows, width), 'dp', spl...]
    all_to_all x3 -> x0, starting transfers between devices: 23 us -> none  [the longest x1 11.5 us: on_device(): lax.all_to_all(wanted, 'dp', split_axis=0, concat_axis=0, tiled=True)]
    unnamed x19 -> x12, local copies, waits for them, and re-layouts: 23.8 us -> 14 us
    div x2 -> x0, other arithmetic: 9.65 us -> none  [the longest x1 6.42 us: on_device(): sum_qkv / total]
    mul x0 -> x1, local copies, waits for them, and re-layouts: none -> 9.6 us  [on_device(): sums = sums.transpose(1, 0, 2).reshape(width, 4 * width).astype(F32) * share]
    slice x0 -> x2, local copies, waits for them, and re-layouts: none -> 8.2 us  [the longest x1 6.38 us: on_device(): sums[:, :3 * width]]
  transfers between devices with their start and end apart: 4 -> 0, of which waited for: 3 -> 0; matrix products, arithmetic and copies ran while one was open for 3% -> 0% of each run, Pallas kernels for 0% -> 0%
where the time goes in v2:
time: 223 us; the launch traced here: 222 us
  Pallas kernels  178 us (80%)
  local copies, waits for them, and re-layouts  35.5 us (16%)
  other arithmetic  7.67 us (3%)
    pallas_call x1, Pallas kernels, reduce(): pl.pallas_call(reduce_kernel, out_shape=(jax.ShapeDtypeStruct(grads.shape...  82.3 us
    pallas_call x1, Pallas kernels, attention(): pl.pallas_call(attention_kernel, out_shape=(shape((rows // 16, 1, 128), F...  60.3 us
    pallas_call x1, Pallas kernels, fetch(): pl.pallas_call(fetch_kernel, out_shape=(jax.ShapeDtypeStruct((3 * rows, w...  35.6 us
    unnamed x12, local copies, waits for them, and re-layouts  14 us
    mul x1, local copies, waits for them, and re-layouts, on_device(): sums = sums.transpose(1, 0, 2).reshape(width, 4 * width).astype(F32) * share  9.6 us
    mul x1, other arithmetic, on_device(): sums = sums.transpose(1, 0, 2).reshape(width, 4 * width).astype(F32) * share  6.89 us
    slice x1, local copies, waits for them, and re-layouts, on_device(): sums[:, :3 * width]  6.38 us

profile of v2, /device:TPU:1, one launch (start us, length us, event | category | flops | bytes accessed | tf_op | source)
XLA Modules:
  0.0 222.0 jit_solution(1766983414368616487)
XLA Ops:
  0.7 0.7 add_add_fusion
  1.4 1.3 reshape.65.gain_ref
  2.6 1.3 reshape.66.bias_ref
  3.9 0.1 copy.19
  4.0 0.1 broadcast_in_dim.24
  4.1 0.1 broadcast_select_fusion
  4.1 0.1 select_n.23.need_ref
  4.2 0.0 copy-start.1
  4.2 1.0 copy-done.1
  5.2 35.6 %fetch_negatives.1 = (bf16[768,768]{1,0:T(8,128)(2,1)S(1)}, s32[128,1,128]{2,1,0:T(1,128)S(1)}) custom-call(bf16[256,768]{1,0:T(8,128)(2,1)S(1)} %bitcast.11, s32[1,128]{1,0:T(1,128)S(1)} %select_n.23.need_ref), custom_call_target="tpu_custom_call" | custom-call | tf_op jit(solution)/shard_map/fetch_negatives/pallas_call | solution.py:352
  40.8 0.0 copy-start
  40.8 1.0 copy-done
  41.8 0.0 copy-start.2
  41.8 0.6 copy-done.2
  42.5 60.3 %pair_attention.1 = (f32[48,1,128]{2,1,0:T(1,128)}, bf16[256,768]{1,0:T(8,128)(2,1)}, f32[256,768]{1,0:T(8,128)}, bf16[512,768]{1,0:T(8,128)(2,1)}, bf16[12,768,256]{2,1,0:T(8,128)(2,1)}) custom-call(s32[16]{0:T(128)} %lens.1, f32[2]{0:T(128)} %ibias.1, bf16[768,768]{1,0:T(8,128)(2,1)} %copy-done, bf16[256,768]{1,0:T(8,128)(2,1)} %bitcast.14, ...), custom_call_target="tpu_custom_call" | custom-call | tf_op jit(solution)/shard_map/pair_attention/pallas_call | solution.py:192
  102.7 0.8 copy.20
  103.5 0.1 reshape_squeeze.3
  103.6 0.7 copy.22
  104.3 82.3 %sum_gradients.1 = (bf16[12,768,256]{2,1,0:T(8,128)(2,1)}, bf16[256,768]{1,0:T(8,128)(2,1)}) custom-call(bf16[12,768,256]{2,1,0:T(8,128)(2,1)} %get-tuple-element.17.g_ref, bf16[512,768]{1,0:T(8,128)(2,1)} %get-tuple-element.18.back_ref, f32[256,768]{1,0:T(8,128)} %get-tuple-element.19.own_ref, s32[128,1,128]{2,1,0:T(1,128)} %copy-done.2), custom_call_target="tpu_custom_call" | custom-call | tf_op jit(solution)/shard_map/sum_gradients/pallas_call | solution.py:594
  186.6 6.9 %multiply_bitcast_fusion = f32[768,12,256]{2,0,1:T(8,128)} fusion(bf16[12,768,256]{2,1,0:T(8,128)(2,1)} %get-tuple-element.22), kind=kLoop, calls=%fused_computation | loop fusion | flops 4718592 | bytes 14155776 | tf_op jit(solution)/shard_map/mul | solution.py:639
  193.5 9.6 %copy.21 = f32[768,12,256]{0,2,1:T(8,128)} copy(f32[768,12,256]{2,0,1:T(8,128)} %multiply_bitcast_fusion) | data formatting | bytes 18874368 | tf_op jit(solution)/shard_map/mul | solution.py:639
  203.1 1.8 slice.13
  204.9 6.4 %slice.12 = f32[768,2304]{0,1:T(8,128)} slice(f32[768,3072]{0,1:T(8,128)} %bitcast.13), slice={[0:768], [0:2304]} | slice | bytes 14155776 | tf_op jit(solution)/shard_map/slice | solution.py:644
  211.3 8.0 %copy.23 = f32[768,2304]{1,0:T(8,128)} copy(f32[768,2304]{0,1:T(8,128)} %slice.12) | data formatting | bytes 14155776
  219.3 0.0 copy-start.3
  219.3 1.9 copy.24
  221.2 0.0 copy-done.3
  221.2 0.7 copy.26
  (1 shorter events, 0.0 us)
Async XLA Ops:
  4.2 1.0 copy-start.1
  40.8 1.0 copy-start
  41.8 0.6 copy-start.2
  219.3 1.9 copy-start.3

commit v3 on v1

v3 whole, which is shorter than its diff:
```python
import math
import jax
import jax.numpy as jnp
from jax import lax
from jax.experimental import pallas as pl
from jax.experimental.pallas import tpu as pltpu
from jax.sharding import PartitionSpec as P

F32 = jnp.float32
BF = jnp.bfloat16
NN = (((1,), (0,)), ((), ()))
NT = (((1,), (1,)), ((), ()))
TN = (((0,), (0,)), ((), ()))


def mm(a, b, dims):
    return lax.dot_general(a, b, dims, preferred_element_type=F32)


HOLDERS = 48
PIECE = 256
MESH = pl.DeviceIdType.MESH


def place():
    me = lax.axis_index("dp")
    return me, me // 32, (me // 8) % 4, (me // 2) % 4, me % 2


def device_at(z, y, x, core):
    return ((z * 4 + y) * 4 + x) * 2 + core


def holder(piece):
    line, k = piece // 3, piece % 3
    z, y = line // 4, line % 4
    return device_at(z, y, (k + 8 - y - z) % 4, piece % 2)


def held_piece():
    me, z, y, x, core = place()
    k = (x + y + z) % 4
    piece = (z * 4 + y) * 3 + k
    return piece, (k < 3) & (core == piece % 2)


def one_hot(mask):
    return jnp.where(mask, 1.0, 0.0).astype(BF)


def swap_rows(outer, inner):
    n = outer * inner
    to = lax.broadcasted_iota(jnp.int32, (n, n), 0)
    source = lax.broadcasted_iota(jnp.int32, (n, n), 1)
    return one_hot(source == lax.rem(to, outer) * inner + lax.div(to, outer))


def pair_kernel(
    lens, ibias, need_ref, q_ref, t_ref, w_ref, wo_ref, gain_ref, bias_ref, iw_ref,
    logits_ref, gtext_ref, query_ref, sum_ref,
    x, qkv, tkv, ctx, gh, ga, gc, gqkv, gt, prob, own_grad, back, grads,
    table, pieces, held, picked, arrived, back_pieces, back_held, totals, back_arrived,
    half_in, in1, sum1, in2, sum2, in3,
    ready, index_send, index_sem, piece_send, held_sem, pick_send, pick_sem,
    back_send, back_sem, total_send, total_sem,
    half_send, half_recv, s_send, s_recv, a_send, a_recv, twin_send, twin_recv,
):
    rows, width = x.shape
    me, z, y, pos_x, core = place()
    mine, holding = held_piece()
    spots = (pos_x, y, z)
    peers, images = held.shape[0], held.shape[1]
    slots = arrived.shape[1]
    pairs_of_heads = width // 128
    unit = 96
    units = rows // unit
    scale = 1.0 / math.sqrt(64.0)
    col = 256
    thirds = range(3)

    def along(axis, step):
        at = [pos_x, y, z]
        at[axis] = (at[axis] + step) % 4
        return device_at(at[2], at[1], at[0], core)

    def axis_of(t, stage):
        return (t + stage) % 3

    twin = me + 1 - 2 * core
    mine_rows = pl.ds(pl.multiple_of(core * 384, 128), 384)
    twin_rows = pl.ds(pl.multiple_of(384 - core * 384, 128), 384)

    def remote(source, target, send, recv, device):
        return pltpu.make_async_remote_copy(
            src_ref=source, dst_ref=target, send_sem=send, recv_sem=recv,
            device_id=(device,), device_id_type=MESH)

    def greet(semaphore, axis):
        for d in (1, 2, 3):
            pl.semaphore_signal(semaphore, inc=1, device_id=(along(axis, d),), device_id_type=MESH)

    barrier = pltpu.get_barrier_semaphore()
    for axis in range(3):
        greet(barrier, axis)
    pl.semaphore_signal(barrier, inc=1, device_id=(twin,), device_id_type=MESH)
    pl.semaphore_wait(barrier, 10)

    pl.semaphore_signal(ready.at[3], inc=1, device_id=(twin,), device_id_type=MESH)
    swapped = mm(swap_rows(images, 16), q_ref[...], NN).astype(BF)
    for r in range(16):
        for k in range(3):
            pieces[r * 3 + k] = swapped[r * images : (r + 1) * images, k * PIECE : (k + 1) * PIECE]
    pl.semaphore_wait(ready.at[3], 1)
    greet(ready.at[0], 0)

    def tkv_step(j, _):
        c = pl.ds(pl.multiple_of(j * col, col), col)
        cw = pl.ds(pl.multiple_of(j * col + width, col), col)
        tkv[:, c] = mm(t_ref[...], w_ref[:, cw], NN).astype(BF)
        return 0

    lax.fori_loop(0, 2, tkv_step, 0)
    pl.semaphore_wait(ready.at[0], 3)
    greet(ready.at[1], 1)
    lax.fori_loop(2, 4, tkv_step, 0)
    pl.semaphore_wait(ready.at[1], 3)
    greet(ready.at[2], 2)
    lax.fori_loop(4, 6, tkv_step, 0)
    pl.semaphore_wait(ready.at[2], 3)

    def spread(i, _):
        piece = (i + me) % HOLDERS
        target = holder(piece)

        @pl.when(target != me)
        def _():
            remote(need_ref, table.at[me], index_send, index_sem, target).start()
            remote(pieces.at[piece], held.at[me], piece_send, held_sem, target).start()

        @pl.when(target == me)
        def _():
            pltpu.make_async_copy(need_ref, table.at[me], index_sem).start()
            pltpu.make_async_copy(pieces.at[piece], held.at[me], held_sem).start()

        return 0

    lax.fori_loop(0, HOLDERS, spread, 0)

    def own_step(j, _):
        c = pl.ds(pl.multiple_of(j * col, col), col)
        got = mm(q_ref[...], w_ref[:, c], NN).astype(BF)
        for i in range(images):
            qkv[i * 48 : i * 48 + 16, c] = got[i * 16 : (i + 1) * 16]
        return 0

    lax.fori_loop(0, 3 * width // col, own_step, 0)

    @pl.when(holding)
    def _():
        pltpu.make_async_copy(table, table, index_sem).wait()
        pltpu.make_async_copy(held, held, held_sem).wait()
        lanes = lax.broadcasted_iota(jnp.int32, (slots, 128), 1)
        lines = lax.broadcasted_iota(jnp.int32, (slots, 128), 0)
        ids = lax.broadcasted_iota(jnp.int32, (1, 2048), 1).astype(F32) + 1.0
        values = held.reshape(2048, PIECE)

        def pick(g, _):
            columns = []
            for b in range(8):
                row = table[g * 8 + b].astype(F32)
                eye = lanes == lines + 32 * (b % 4)
                columns.append(jnp.sum(jnp.where(eye, row, 0.0), axis=-1, keepdims=True))
            hot = one_hot(jnp.concatenate(columns, axis=0) == ids)
            chosen = mm(hot, values[...], NN).astype(BF)
            for b in range(8):
                target = g * 8 + b
                picked[target] = chosen[b * slots : (b + 1) * slots]

                @pl.when(target != me)
                def _():
                    remote(picked.at[target], arrived.at[mine], pick_send, pick_sem, target).start()

                @pl.when(target == me)
                def _():
                    pltpu.make_async_copy(picked.at[target], arrived.at[mine], pick_sem).start()

            return 0

        lax.fori_loop(0, peers // 8, pick, 0)

    swap = swap_rows(16, slots)
    pltpu.make_async_copy(arrived, arrived, pick_sem).wait()
    for k in range(3):
        c = slice(k * PIECE, (k + 1) * PIECE)
        stacked = jnp.concatenate([arrived[r * 3 + k] for r in range(16)], axis=0)
        block = mm(swap, stacked, NN).astype(BF)
        for i in range(images):
            x[i * 48 : i * 48 + 16, c] = q_ref[i * 16 : (i + 1) * 16, c]
            x[i * 48 + 16 : i * 48 + 48, c] = block[i * 32 : (i + 1) * 32]
            back[i * 32 : (i + 1) * 32, c] = block[i * 32 : (i + 1) * 32]

    def negative_step(j, _):
        c = pl.ds(pl.multiple_of(j * col, col), col)
        got = mm(back[...], w_ref[:, c], NN).astype(BF)
        for i in range(images):
            qkv[i * 48 + 16 : i * 48 + 48, c] = got[i * 32 : (i + 1) * 32]
        return 0

    lax.fori_loop(0, 3 * width // col, negative_step, 0)

    lane = lax.broadcasted_iota(jnp.int32, (1, 128), 1)
    low = lane < 64

    def by_head(a):
        zero = jnp.zeros_like(a)
        return jnp.concatenate([jnp.where(low, a, zero), jnp.where(low, zero, a)], axis=0)

    def keys_of(g, j, first):
        r = pl.ds(pl.multiple_of(g * unit, 32), unit)
        tr = pl.ds(pl.multiple_of(g * 32, 32), 32)
        image = qkv[r, first + j * 128 : first + (j + 1) * 128]
        text = tkv[tr, first - width + j * 128 : first - width + (j + 1) * 128]
        return by_head(jnp.concatenate([image, text], axis=0))

    def forward(g, _):
        r = pl.ds(pl.multiple_of(g * unit, 32), unit)
        rowi = lax.broadcasted_iota(jnp.int32, (unit, 128), 0)
        lanei = lax.broadcasted_iota(jnp.int32, (unit, 128), 1)
        first = rowi < 48
        start = jnp.where(first, 96, 112)
        live = jnp.where(first, lens[2 * g], lens[2 * g + 1])
        block = rowi - lax.rem(rowi, 16)
        valid = ((lanei >= block) & (lanei < block + 16)) | ((lanei >= start) & (lanei < start + live))
        for j in range(pairs_of_heads):
            q = qkv[r, j * 128 : (j + 1) * 128]
            s = mm(q, keys_of(g, j, width), NT) * scale
            parts = []
            for h in range(2):
                sh = jnp.where(valid, s[:, h * 128 : (h + 1) * 128], -1e30)
                e = jnp.exp(sh - jnp.max(sh, axis=-1, keepdims=True))
                parts.append(e * (1.0 / jnp.sum(e, axis=-1, keepdims=True)))
            p = jnp.concatenate(parts, axis=1)
            prob[r, j * 256 : (j + 1) * 256] = p
            ctx[r, j * 128 : (j + 1) * 128] = mm(p.astype(BF), keys_of(g, j, 2 * width), NN).astype(BF)
        return 0

    lax.fori_loop(0, units, forward, 0)

    gw0 = gain_ref[...].reshape(1, -1) * iw_ref[0:1, :]
    gw1 = gain_ref[...].reshape(1, -1) * iw_ref[1:2, :]
    slope = (gw1 - gw0) * (1.0 / 16.0)
    slope_mean = jnp.mean(slope)
    base0 = jnp.sum(bias_ref[...].reshape(1, -1) * iw_ref[0:1, :]) + ibias[0]
    base1 = jnp.sum(bias_ref[...].reshape(1, -1) * iw_ref[1:2, :]) + ibias[1]
    part = 192
    tails = part // 16

    def tail(m, _):
        r = pl.ds(pl.multiple_of(m * part, 64), part)
        h = x[r, :].astype(F32) + mm(ctx[r, :], wo_ref[...], NN)
        center = h - jnp.mean(h, axis=-1, keepdims=True)
        spread = jnp.mean(center * center, axis=-1, keepdims=True)
        rstd = lax.rsqrt(spread + 1e-6)
        xhat = center * rstd
        a0 = jnp.sum(xhat * gw0, axis=-1, keepdims=True)
        a1 = jnp.sum(xhat * gw1, axis=-1, keepdims=True)
        l0 = jnp.mean(a0.reshape(tails, 16, 1), axis=1, keepdims=True) + base0
        l1 = jnp.mean(a1.reshape(tails, 16, 1), axis=1, keepdims=True) + base1
        kind = lax.rem(lax.broadcasted_iota(jnp.int32, (tails, 1, 1), 0), 3)
        sign = jnp.where(kind == 0, -1.0, 1.0)
        g1 = sign / (1.0 + jnp.exp(-sign * (l1 - l0)))
        g1 = jnp.broadcast_to(g1, (tails, 16, 1)).reshape(part, 1)
        moved = (a1 - a0) * (1.0 / (16.0 * width))
        g = (rstd * g1) * ((slope - slope_mean) - xhat * moved)
        gh[r, :] = g
        low_g = g.astype(BF)
        ga[r, :] = low_g
        gc[r, :] = mm(low_g, wo_ref[...], NT).astype(BF)
        both = jnp.where(lax.broadcasted_iota(jnp.int32, (tails, 1, 128), 2) == 0, l0, l1)
        logits_ref[pl.ds(m * tails, tails)] = both
        return 0

    lax.fori_loop(0, rows // part, tail, 0)

    def backward(g, _):
        r = pl.ds(pl.multiple_of(g * unit, 32), unit)
        tr = pl.ds(pl.multiple_of(g * 32, 32), 32)
        for j in range(pairs_of_heads):
            c = slice(j * 128, (j + 1) * 128)
            gcj = gc[r, c]
            gp = mm(gcj, keys_of(g, j, 2 * width), NT)
            p = prob[r, j * 256 : (j + 1) * 256]
            gs, pl_low = [], []
            for h in range(2):
                ph = p[:, h * 128 : (h + 1) * 128]
                gph = gp[:, h * 128 : (h + 1) * 128]
                mean = jnp.sum(gph * ph, axis=-1, keepdims=True)
                gs.append((ph * (gph - mean) * scale).astype(BF))
                pl_low.append(ph.astype(BF))
            gq = mm(jnp.concatenate(gs, axis=1), keys_of(g, j, width), NN)
            gk = mm(jnp.concatenate(gs, axis=0), by_head(qkv[r, c]), TN).astype(BF)
            gv = mm(jnp.concatenate(pl_low, axis=0), by_head(gcj), TN).astype(BF)
            gqkv[r, c] = gq.astype(BF)
            gqkv[r, width + j * 128 : width + (j + 1) * 128] = gk[:96]
            gqkv[r, 2 * width + j * 128 : 2 * width + (j + 1) * 128] = gv[:96]
            gt[tr, c] = gk[96:]
            gt[tr, width + j * 128 : width + (j + 1) * 128] = gv[96:]
        return 0

    lax.fori_loop(0, units, backward, 0)

    def to_rows(m, _):
        r = pl.ds(pl.multiple_of(m * part, 64), part)
        g = mm(gqkv[r, :], w_ref[...], NT) + gh[r, :]
        for k in range(part // 48):
            own = pl.ds(pl.multiple_of(m * (part // 3) + k * 16, 16), 16)
            neg = pl.ds(pl.multiple_of(m * (2 * part // 3) + k * 32, 32), 32)
            own_grad[own, :] = g[k * 48 : k * 48 + 16]
            back[neg, :] = g[k * 48 + 16 : k * 48 + 48].astype(BF)
        return 0

    lax.fori_loop(0, rows // part, to_rows, 0)


    swapped = mm(swap_rows(slots, 16), back[...], NN).astype(BF)
    for r in range(16):
        for k in range(3):
            back_pieces[r * 3 + k] = swapped[r * slots : (r + 1) * slots, k * PIECE : (k + 1) * PIECE]

    def spread_back(i, _):
        piece = (i + me) % HOLDERS
        target = holder(piece)

        @pl.when(target != me)
        def _():
            remote(back_pieces.at[piece], back_held.at[me], back_send, back_sem, target).start()

        @pl.when(target == me)
        def _():
            pltpu.make_async_copy(back_pieces.at[piece], back_held.at[me], back_sem).start()

        return 0

    lax.fori_loop(0, HOLDERS, spread_back, 0)

    def half_copy(j):
        return remote(grads.at[j, twin_rows], half_in.at[j], half_send.at[j], half_recv.at[j], twin)

    def weight_step(j, _):
        c = pl.ds(pl.multiple_of(j * col, col), col)
        grads[j] = mm(x[...], gqkv[:, c], TN).astype(BF)
        half_copy(j).start()
        return 0

    lax.fori_loop(0, width // col, weight_step, 0)

    def weight_text_step(j, _):
        c = pl.ds(pl.multiple_of(j * col, col), col)
        ct = pl.ds(pl.multiple_of(j * col - width, col), col)
        grads[j] = (mm(x[...], gqkv[:, c], TN) + mm(t_ref[...], gt[:, ct], TN)).astype(BF)
        half_copy(j).start()
        return 0

    lax.fori_loop(width // col, 3 * width // col, weight_text_step, 0)

    def out_step(j, _):
        c = pl.ds(pl.multiple_of(j * col - 3 * width, col), col)
        grads[j] = mm(ctx[...], ga[:, c], TN).astype(BF)
        half_copy(j).start()
        return 0

    lax.fori_loop(3 * width // col, 4 * width // col, out_step, 0)

    sends = []

    def start(copy):
        copy.start()
        sends.append(copy)

    one = {}
    for t in thirds:
        axis = axis_of(t, 0)

        def add_half(k, _, t=t):
            half_copy(4 * t + k).wait_recv()
            own = grads[4 * t + k, mine_rows, :].astype(F32)
            half_in[4 * t + k] = (own + half_in[4 * t + k].astype(F32)).astype(BF)
            return 0

        lax.fori_loop(0, 4, add_half, 0)
        for d in (1, 2, 3):
            to = (spots[axis] + d) % 4
            one[t, d] = remote(half_in.at[4 * t + to], in1.at[t, d - 1],
                               s_send.at[t, d], s_recv.at[t, d], along(axis, d))
            start(one[t, d])

    @pl.when(holding)
    def _():
        pltpu.make_async_copy(back_held, back_held, back_sem).wait()
        values = back_held.reshape(peers * slots, PIECE)
        ids = lax.broadcasted_iota(jnp.int32, (256, 128), 0).astype(F32) + 1.0
        rows = [
            table[4 * b].astype(F32) + table[4 * b + 1].astype(F32)
            + table[4 * b + 2].astype(F32) + table[4 * b + 3].astype(F32)
            for b in range(peers // 4)
        ]

        def add_up(g, _):
            shift = (g * 256).astype(F32)
            hot = jnp.concatenate([one_hot(ids == row - shift) for row in rows], axis=1)
            total = mm(hot, values[...], NN).astype(BF)
            for b in range(16):
                target = g * 16 + b
                totals[target] = total[b * images : (b + 1) * images]

                @pl.when(target != me)
                def _():
                    remote(totals.at[target], back_arrived.at[mine], total_send, total_sem, target).start()

                @pl.when(target == me)
                def _():
                    pltpu.make_async_copy(totals.at[target], back_arrived.at[mine], total_sem).start()

            return 0

        lax.fori_loop(0, peers // 16, add_up, 0)


    gtext_ref[...] = mm(gt[...], w_ref[:, width:], NT).astype(BF)

    two = {}
    for t in thirds:
        axis, after = axis_of(t, 0), axis_of(t, 1)
        for d in (1, 2, 3):
            one[t, d].wait_recv()
        total = half_in[4 * t + spots[axis]].astype(F32)
        for d in range(3):
            total += in1[t, d].astype(F32)
        sum1[t] = total.astype(BF)
        for d in (1, 2, 3):
            to = (spots[after] + d) % 4
            two[t, d] = remote(sum1.at[t, pl.ds(pl.multiple_of(to * 96, 32), 96)], in2.at[t, d - 1],
                               s_send.at[t, 3 + d], s_recv.at[t, 3 + d], along(after, d))
            start(two[t, d])

    def corner(ref, first, spot):
        rows = pl.ds(pl.multiple_of(first + (spot // 2) * 48, 16), 48)
        return ref.at[rows, pl.ds(pl.multiple_of((spot % 2) * 128, 128), 128)]

    three = {}
    for t in thirds:
        axis, after = axis_of(t, 1), axis_of(t, 2)
        for d in (1, 2, 3):
            two[t, d].wait_recv()
        total = sum1[t, pl.ds(pl.multiple_of(spots[axis] * 96, 32), 96), :].astype(F32)
        for d in range(3):
            total += in2[t, d].astype(F32)
        sum2[t] = total.astype(BF)
        for d in (1, 2, 3):
            to = (spots[after] + d) % 4
            three[t, d] = remote(corner(sum2.at[t], 0, to), in3.at[t, d - 1],
                                 s_send.at[t, 6 + d], s_recv.at[t, 6 + d], along(after, d))
            start(three[t, d])

    last = {}
    for t in thirds:
        axis = axis_of(t, 2)
        for d in (1, 2, 3):
            three[t, d].wait_recv()
        total = corner(sum2.at[t], 0, spots[axis])[...].astype(F32)
        for d in range(3):
            total += in3[t, d].astype(F32)
        block = sum_ref.at[4 * t + spots[axis_of(t, 0)]]
        first = core * 384 + spots[axis_of(t, 1)] * 96
        piece = corner(block, first, spots[axis])
        piece[...] = total.astype(BF)
        for d in (1, 2, 3):
            last[t, d] = remote(piece, piece, a_send.at[t, d], a_recv.at[t, d], along(axis, d))
            start(last[t, d])

    def came(t, stage, ref, d):
        return pltpu.make_async_copy(ref, ref, a_recv.at[t, stage * 3 + d])

    for t in thirds:
        axis = axis_of(t, 1)
        block = sum_ref.at[4 * t + spots[axis_of(t, 0)]]
        first = core * 384 + spots[axis] * 96
        for d in (1, 2, 3):
            came(t, 0, corner(block, first, (spots[axis_of(t, 2)] + 4 - d) % 4), d).wait()
        piece = block.at[pl.ds(pl.multiple_of(first, 32), 96)]
        for d in (1, 2, 3):
            start(remote(piece, piece, a_send.at[t, 3 + d], a_recv.at[t, 3 + d], along(axis, d)))

    for t in thirds:
        axis = axis_of(t, 0)
        block = sum_ref.at[4 * t + spots[axis]]
        for d in (1, 2, 3):
            spot = (spots[axis_of(t, 1)] + 4 - d) % 4
            came(t, 1, block.at[pl.ds(pl.multiple_of(core * 384 + spot * 96, 32), 96)], d).wait()
        piece = block.at[mine_rows]
        start(remote(piece, piece, twin_send.at[t, 0], twin_recv.at[t, 0], twin))
        for d in (1, 2, 3):
            start(remote(piece, piece, a_send.at[t, 6 + d], a_recv.at[t, 6 + d], along(axis, d)))

    for t in thirds:
        axis = axis_of(t, 0)
        for d in (1, 2, 3):
            piece = sum_ref.at[4 * t + (spots[axis] + 4 - d) % 4, mine_rows]
            came(t, 2, piece, d).wait()
            start(remote(piece, piece, twin_send.at[t, d], twin_recv.at[t, d], twin))


    pltpu.make_async_copy(back_arrived, back_arrived, total_sem).wait()
    swap = swap_rows(16, images)
    for k in range(3):
        c = slice(k * PIECE, (k + 1) * PIECE)
        stacked = jnp.concatenate([back_arrived[r * 3 + k] for r in range(16)], axis=0)
        query_ref[:, c] = (own_grad[:, c] + mm(swap, stacked, NN)).astype(BF)

    for t in thirds:
        for d in range(4):
            other = sum_ref.at[4 * t + (spots[axis_of(t, 0)] + 4 - d) % 4, twin_rows]
            pltpu.make_async_copy(other, other, twin_recv.at[t, d]).wait()
    for copy in sends:
        copy.wait_send()

    def half_sent(j, _):
        half_copy(j).wait_send()
        return 0

    lax.fori_loop(0, 4 * width // col, half_sent, 0)

    def sent(ref, count, semaphore):
        pltpu.make_async_copy(ref.at[0:count], ref.at[0:count], semaphore).wait()

    @pl.when(holding)
    def _():
        sent(pieces, HOLDERS - 1, piece_send)
        sent(table, HOLDERS - 1, index_send)
        sent(picked, peers - 1, pick_send)
        sent(back_pieces, HOLDERS - 1, back_send)
        sent(totals, peers - 1, total_send)

    @pl.when(jnp.logical_not(holding))
    def _():
        sent(pieces, HOLDERS, piece_send)
        sent(table, HOLDERS, index_send)
        sent(back_pieces, HOLDERS, back_send)


def pair_losses(lens, ib, need, queries, texts, w, wo, gain, bias, iw, peers):
    own, width = queries.shape
    rows, trows = 3 * own, texts.shape[0]
    images = own // 16
    vmem = pl.BlockSpec(memory_space=pltpu.VMEM)
    smem = pl.BlockSpec(memory_space=pltpu.SMEM)
    shape = jax.ShapeDtypeStruct
    dma = pltpu.SemaphoreType.DMA
    return pl.pallas_call(
        pair_kernel,
        out_shape=(
            shape((rows // 16, 1, 128), F32),
            shape((trows, width), BF),
            shape((own, width), BF),
            shape((12, width, 256), BF),
        ),
        in_specs=[smem, smem] + [vmem] * 8,
        out_specs=(vmem,) * 4,
        scratch_shapes=[
            pltpu.VMEM((rows, width), BF),
            pltpu.VMEM((rows, 3 * width), BF),
            pltpu.VMEM((trows, 2 * width), BF),
            pltpu.VMEM((rows, width), BF),
            pltpu.VMEM((rows, width), F32),
            pltpu.VMEM((rows, width), BF),
            pltpu.VMEM((rows, width), BF),
            pltpu.VMEM((rows, 3 * width), BF),
            pltpu.VMEM((trows, 2 * width), BF),
            pltpu.VMEM((rows, 2 * width), F32),
            pltpu.VMEM((own, width), F32),
            pltpu.VMEM((2 * own, width), BF),
            pltpu.VMEM((12, width, 256), BF),
            pltpu.VMEM((peers, 1, 128), jnp.int32),
            pltpu.VMEM((HOLDERS, images, PIECE), BF),
            pltpu.VMEM((peers, images, PIECE), BF),
            pltpu.VMEM((peers, 2 * images, PIECE), BF),
            pltpu.VMEM((HOLDERS, 2 * images, PIECE), BF),
            pltpu.VMEM((HOLDERS, 2 * images, PIECE), BF),
            pltpu.VMEM((peers, 2 * images, PIECE), BF),
            pltpu.VMEM((peers, images, PIECE), BF),
            pltpu.VMEM((HOLDERS, images, PIECE), BF),
            pltpu.VMEM((12, 384, 256), BF),
            pltpu.VMEM((3, 3, 384, 256), BF),
            pltpu.VMEM((3, 384, 256), BF),
            pltpu.VMEM((3, 3, 96, 256), BF),
            pltpu.VMEM((3, 96, 256), BF),
            pltpu.VMEM((3, 3, 48, 128), BF),
            pltpu.SemaphoreType.REGULAR((4,)),
            dma, dma, dma, dma, dma, dma, dma, dma, dma, dma,
            dma((12,)), dma((12,)), dma((3, 10)), dma((3, 10)), dma((3, 10)), dma((3, 10)),
            dma((3, 4)), dma((3, 4)),
        ],
        compiler_params=pltpu.CompilerParams(
            vmem_limit_bytes=63 * 1024 * 1024, has_side_effects=True, collective_id=0
        ),
        name="pair_losses",
    )(lens, ib, need, queries, texts, w, wo, gain, bias, iw.T)


def widen_kernel(share, sum_ref, qkv_ref, out_ref):
    j = pl.program_id(0)

    @pl.when(j < 9)
    def _():
        qkv_ref[...] = sum_ref[0].astype(F32) * share

    @pl.when(j >= 9)
    def _():
        out_ref[...] = sum_ref[0].astype(F32) * share


def widen(sums, share):
    width = sums.shape[1]
    return pl.pallas_call(
        lambda *refs: widen_kernel(share, *refs),
        grid=(12,),
        out_shape=(
            jax.ShapeDtypeStruct((width, 3 * width), F32),
            jax.ShapeDtypeStruct((width, width), F32),
        ),
        in_specs=[pl.BlockSpec((1, width, 256), lambda j: (j, 0, 0))],
        out_specs=(
            pl.BlockSpec((width, 256), lambda j: (0, jnp.minimum(j, 8))),
            pl.BlockSpec((width, 256), lambda j: (0, jnp.maximum(j - 9, 0))),
        ),
        name="widen",
    )(sums)


def on_device(
    text_states, text_len, query_states, neg_owner, neg_slot,
    projection_weight, output_weight, ln_gain, ln_bias, itm_weight, itm_bias,
):
    captions, query_rows, width = query_states.shape
    peers = lax.axis_size("dp")
    me = lax.axis_index("dp")
    wanted = (captions * neg_owner + neg_slot + 1).reshape(1, 2 * captions)
    group = jnp.arange(4)[:, None] == me % 4
    need = jnp.where(group, wanted, 0).reshape(1, 128)
    logits, grad_text, grad_query, sums = pair_losses(
        text_len, itm_bias, need, query_states.reshape(-1, width), text_states.reshape(-1, width),
        projection_weight, output_weight, ln_gain, ln_bias, itm_weight, peers,
    )
    sum_qkv, sum_out = widen(sums, 1.0 / (captions * peers))
    return (
        logits[:, 0, :2].reshape(captions, 3, 2),
        grad_text.reshape(text_states.shape),
        grad_query.reshape(query_states.shape),
        sum_qkv,
        sum_out,
    )


def solution(mesh):
    rows = P("dp", None, None)
    placed = (rows, P("dp"), rows, P("dp", None), P("dp", None)) + (P(),) * 6
    return jax.shard_map(
        on_device, mesh=mesh, in_specs=placed, out_specs=(rows, rows, rows, P(), P()), check_vma=False
    )
```

time: 448 us -> 166 us (0.37)
  waiting for transfers between devices: 301 us -> 0 us
  Pallas kernels: 61.8 us -> 161 us
  local copies, waits for them, and re-layouts: 28.6 us -> 3.91 us
  starting transfers between devices: 23 us -> 0 us
  between operations: 14.2 us -> 0.68 us
  other arithmetic: 12.5 us -> 0.78 us
  matrix products: 5.96 us -> 0 us
    psum x1 -> x0, waiting for transfers between devices: 218 us -> none  [on_device(): sum_qkv, sum_out = lax.psum((dw, dwo), 'dp')]
    pallas_call x1 -> x2, Pallas kernels: 61.8 us -> 161 us  [the longest x1 151 us: pair_losses(): pl.pallas_call(pair_kernel, out_shape=(shape((rows // 16, 1, 128), F32),...]
    all_to_all x3 -> x0, waiting for transfers between devices: 82.6 us -> none  [the longest x1 74.2 us: on_device(): lax.all_to_all(outgoing.reshape(peers, CAP, query_rows, width), 'dp', spl...]
    all_to_all x3 -> x0, starting transfers between devices: 23 us -> none  [the longest x1 11.5 us: on_device(): lax.all_to_all(wanted, 'dp', split_axis=0, concat_axis=0, tiled=True)]
    unnamed x19 -> x7, local copies, waits for them, and re-layouts: 23.8 us -> 2.18 us
    div x2 -> x0, other arithmetic: 9.65 us -> none  [the longest x1 6.42 us: on_device(): sum_qkv / total]
    dot_general x4 -> x0, matrix products: 5.96 us -> none  [the longest x1 1.89 us: on_device(): jnp.dot(take.T, back.reshape(requests, -1), preferred_element_type=F32)]
  transfers between devices with their start and end apart: 4 -> 0, of which waited for: 3 -> 0; matrix products, arithmetic and copies ran while one was open for 3% -> 0% of each run, Pallas kernels for 0% -> 0%
where the time goes in v3:
time: 166 us
  Pallas kernels  161 us (97%)
  local copies, waits for them, and re-layouts  3.91 us (2%)
    pallas_call x1, Pallas kernels, pair_losses(): pl.pallas_call(pair_kernel, out_shape=(shape((rows // 16, 1, 128), F32),...  151 us
    pallas_call x1, Pallas kernels, widen(): pl.pallas_call(lambda *refs: widen_kernel(share, *refs), grid=(12,), out_...  9.68 us

profile of v3, /device:TPU:1, one launch (start us, length us, event | category | flops | bytes accessed | tf_op | source)
XLA Modules:
  0.0 165.9 jit_solution(12046268520618661225)
XLA Ops:
  0.7 0.7 add_add_fusion
  1.4 0.1 copy.19
  1.4 0.1 broadcast_in_dim.24
  1.5 0.1 broadcast_select_fusion
  1.6 0.6 select_n.23.need_ref
  2.2 150.9 %pair_losses.1 = (f32[48,1,128]{2,1,0:T(1,128)}, bf16[256,768]{1,0:T(8,128)(2,1)}, bf16[256,768]{1,0:T(8,128)(2,1)}, bf16[12,768,256]{2,1,0:T(8,128)(2,1)}) custom-call(s32[16]{0:T(128)} %lens.1, f32[2]{0:T(128)} %ibias.1, s32[1,128]{1,0:T(1,128)} %select_n.23.need_ref, bf16[256,768]{1,0:T(8,128)(2,1)} %bitcast.8, bf16[256,768]{1,0:T(8,128)(2,1)} %bitcast.9, ...), custom_call_target="tpu_custom_call" | custom-call | tf_op jit(solution)/shard_map/pair_losses/pallas_call | solution.py:559
  153.1 0.0 copy-start.1
  153.1 0.0 copy-start
  153.1 0.9 copy.20
  154.0 0.1 reshape_squeeze.3
  154.1 0.7 copy.21
  154.8 9.7 %widen.1 = (f32[768,2304]{1,0:T(8,128)}, f32[768,768]{1,0:T(8,128)}) custom-call(bf16[12,768,256]{2,1,0:T(8,128)(2,1)} %get-tuple-element.14.refs_0_), custom_call_target="tpu_custom_call" | custom-call | tf_op jit(solution)/shard_map/widen/pallas_call | solution.py:624
  164.4 0.0 copy-done.1
  164.5 0.7 copy.24
  165.2 0.0 copy-done
  165.2 0.7 copy.25
  (1 shorter events, 0.0 us)
Async XLA Ops:
  153.1 11.3 %copy-start.1 = (bf16[256,768]{1,0:T(8,128)(2,1)S(1)}, bf16[256,768]{1,0:T(8,128)(2,1)}, u32[]{:S(2)}) copy-start(bf16[256,768]{1,0:T(8,128)(2,1)} %get-tuple-element.12) | copy-start | bytes 1179652
  153.1 12.1 %copy-start = (bf16[256,768]{1,0:T(8,128)(2,1)S(1)}, bf16[256,768]{1,0:T(8,128)(2,1)}, u32[]{:S(2)}) copy-start(bf16[256,768]{1,0:T(8,128)(2,1)} %get-tuple-element.13) | copy-start | bytes 1179652

commit v4 on v3

v4 whole, which is shorter than its diff:
```python
import math
import jax
import jax.numpy as jnp
from jax import lax
from jax.experimental import pallas as pl
from jax.experimental.pallas import tpu as pltpu
from jax.sharding import PartitionSpec as P

F32 = jnp.float32
BF = jnp.bfloat16
NN = (((1,), (0,)), ((), ()))
NT = (((1,), (1,)), ((), ()))
TN = (((0,), (0,)), ((), ()))


def mm(a, b, dims):
    return lax.dot_general(a, b, dims, preferred_element_type=F32)


HOLDERS = 48
PIECE = 256
MESH = pl.DeviceIdType.MESH


def place():
    me = lax.axis_index("dp")
    return me, me // 32, (me // 8) % 4, (me // 2) % 4, me % 2


def device_at(z, y, x, core):
    return ((z * 4 + y) * 4 + x) * 2 + core


def holder(piece, core):
    line, k = piece // 3, piece % 3
    z, y = line // 4, line % 4
    return device_at(z, y, (k + 8 - y - z) % 4, core)


def held_piece():
    me, z, y, x, core = place()
    k = (x + y + z) % 4
    return (z * 4 + y) * 3 + k, k < 3


def one_hot(mask):
    return jnp.where(mask, 1.0, 0.0).astype(BF)


def swap_rows(outer, inner):
    n = outer * inner
    to = lax.broadcasted_iota(jnp.int32, (n, n), 0)
    source = lax.broadcasted_iota(jnp.int32, (n, n), 1)
    return one_hot(source == lax.rem(to, outer) * inner + lax.div(to, outer))


def pair_kernel(
    lens, ibias, need_ref, q_ref, t_ref, w_hbm, wo_hbm, gain_ref, bias_ref, iw_ref,
    logits_ref, gtext_ref, query_ref, sum_ref,
    x, qkv, tkv, ctx, gh, ga, gc, gqkv, gt, gt_own, prob, own_grad, back, grads,
    table, pieces, held, picked, arrived, back_pieces, back_held, partial, twin_partial,
    totals, back_arrived,
    half_in, in1, sum1, in2, sum2, in3,
    w_ref, wo_ref, load_sem, index_send, index_sem, swap_send, swap_recv,
    partial_send, partial_recv, piece_send, held_sem, pick_send, pick_sem,
    back_send, back_sem, total_send, total_sem,
    half_send, half_recv, s_send, s_recv, a_send, a_recv, twin_send, twin_recv,
):
    rows, width = x.shape
    me, z, y, pos_x, core = place()
    mine, holding = held_piece()
    spots = (pos_x, y, z)
    chips, images = held.shape[1], held.shape[2]
    chip = me // 2
    slots = arrived.shape[1]
    pairs_of_heads = width // 128
    unit = 64
    own = q_ref.shape[0]
    scale = 1.0 / math.sqrt(64.0)
    col = 256
    thirds = range(3)

    def along(axis, step):
        at = [pos_x, y, z]
        at[axis] = (at[axis] + step) % 4
        return device_at(at[2], at[1], at[0], core)

    def axis_of(t, stage):
        return (t + stage) % 3

    twin = me + 1 - 2 * core
    mine_rows = pl.ds(pl.multiple_of(core * 384, 128), 384)
    twin_rows = pl.ds(pl.multiple_of(384 - core * 384, 128), 384)

    def remote(source, target, send, recv, device):
        return pltpu.make_async_remote_copy(
            src_ref=source, dst_ref=target, send_sem=send, recv_sem=recv,
            device_id=(device,), device_id_type=MESH)

    barrier = pltpu.get_barrier_semaphore()

    def greet(device):
        pl.semaphore_signal(barrier, inc=1, device_id=(device,), device_id_type=MESH)

    line = me - me % 8
    for d in range(1, 8):
        greet(line + (me + d) % 8)
    for axis in (1, 2):
        for d in (1, 2, 3):
            greet(along(axis, d))

    w_copy = pltpu.make_async_copy(w_hbm, w_ref, load_sem.at[0])
    wo_copy = pltpu.make_async_copy(wo_hbm, wo_ref, load_sem.at[1])
    w_copy.start()
    wo_copy.start()
    swapped = mm(swap_rows(images, 16), q_ref[...], NN).astype(BF)
    for r in range(16):
        for k in range(3):
            pieces[r * 3 + k] = swapped[r * images : (r + 1) * images, k * PIECE : (k + 1) * PIECE]
    table[me] = need_ref[...]
    pl.semaphore_wait(barrier, 13)

    gathers = []

    def gather(rows, device, number):
        copy = remote(table.at[rows], table.at[rows], index_send.at[number], index_sem.at[number], device)
        copy.start()
        gathers.append(copy)

    def gathered(rows, number):
        pltpu.make_async_copy(table.at[rows], table.at[rows], index_sem.at[number]).wait()

    def tkv_step(j, _):
        c = pl.ds(pl.multiple_of(j * col, col), col)
        cw = pl.ds(pl.multiple_of(j * col + width, col), col)
        tkv[:, c] = mm(t_ref[...], w_ref[:, cw], NN).astype(BF)
        return 0

    def own_step(j, _):
        c = pl.ds(pl.multiple_of(j * col, col), col)
        qkv[0:own, c] = mm(q_ref[...], w_ref[:, c], NN).astype(BF)
        return 0

    for d in range(1, 8):
        gather(pl.ds(me, 1), line + (me + d) % 8, d - 1)
    w_copy.wait()
    lax.fori_loop(0, 6, tkv_step, 0)
    for d in range(1, 8):
        gathered(pl.ds(line + (me + 8 - d) % 8, 1), d - 1)
    for d in (1, 2, 3):
        gather(pl.ds(line, 8), along(1, d), 6 + d)
    lax.fori_loop(0, 5, own_step, 0)
    for d in (1, 2, 3):
        gathered(pl.ds((z * 4 + (y + 4 - d) % 4) * 8, 8), 6 + d)
    for d in (1, 2, 3):
        gather(pl.ds(z * 32, 32), along(2, d), 9 + d)
    lax.fori_loop(5, 9, own_step, 0)
    for d in (1, 2, 3):
        gathered(pl.ds(((z + 4 - d) % 4) * 32, 32), 9 + d)

    def spread(i, _):
        piece = (i + me) % HOLDERS
        target = holder(piece, core)

        @pl.when(target != me)
        def _():
            remote(pieces.at[piece], held.at[core, chip], piece_send, held_sem, target).start()

        @pl.when(target == me)
        def _():
            pltpu.make_async_copy(pieces.at[piece], held.at[core, chip], held_sem).start()

        return 0

    lax.fori_loop(0, HOLDERS, spread, 0)
    other = 1 - core

    def swap_copy():
        return remote(held.at[core], held.at[core], swap_send, swap_recv, twin)

    lane = lax.broadcasted_iota(jnp.int32, (1, 128), 1)
    low = lane < 64

    def by_head(a):
        zero = jnp.zeros_like(a)
        return jnp.concatenate([jnp.where(low, a, zero), jnp.where(low, zero, a)], axis=0)

    def spans(negative, u):
        if negative:
            return pl.ds(pl.multiple_of(own + u * unit, 64), unit), pl.ds(pl.multiple_of(u * 32, 32), 32)
        at = pl.ds(pl.multiple_of(u * unit, 64), unit)
        return at, at

    def keys_of(negative, u, j, first):
        r, tr = spans(negative, u)
        parts = [
            qkv[r, first + j * 128 : first + (j + 1) * 128],
            tkv[tr, first - width + j * 128 : first - width + (j + 1) * 128],
        ]
        if negative:
            parts.append(jnp.zeros((32, 128), BF))
        return by_head(jnp.concatenate(parts, axis=0))

    def forward(negative, u):
        r, _ = spans(negative, u)
        rowi = lax.broadcasted_iota(jnp.int32, (unit, 128), 0)
        lanei = lax.broadcasted_iota(jnp.int32, (unit, 128), 1)
        block = rowi - lax.rem(rowi, 16)
        if negative:
            first = rowi < 32
            start = jnp.where(first, 64, 80)
            live = jnp.where(first, lens[2 * u], lens[2 * u + 1])
        else:
            start = block + 64
            live = jnp.where(
                rowi < 32,
                jnp.where(rowi < 16, lens[4 * u], lens[4 * u + 1]),
                jnp.where(rowi < 48, lens[4 * u + 2], lens[4 * u + 3]),
            )
        valid = ((lanei >= block) & (lanei < block + 16)) | ((lanei >= start) & (lanei < start + live))
        heads = range(pairs_of_heads)
        scores = [
            mm(qkv[r, j * 128 : (j + 1) * 128], keys_of(negative, u, j, width), NT) * scale for j in heads
        ]
        probs = []
        for s in scores:
            parts = []
            for h in range(2):
                sh = jnp.where(valid, s[:, h * 128 : (h + 1) * 128], -1e30)
                e = jnp.exp(sh - jnp.max(sh, axis=-1, keepdims=True))
                parts.append(e * (1.0 / jnp.sum(e, axis=-1, keepdims=True)))
            probs.append(jnp.concatenate(parts, axis=1))
        outs = [mm(p.astype(BF), keys_of(negative, u, j, 2 * width), NN) for j, p in zip(heads, probs)]
        for j, p, o in zip(heads, probs, outs):
            prob[r, j * 256 : (j + 1) * 256] = p
            ctx[r, j * 128 : (j + 1) * 128] = o.astype(BF)

    gain = gain_ref[...].reshape(1, -1)
    bias = bias_ref[...].reshape(1, -1)
    gw0 = gain * iw_ref[0:1, :]
    gw1 = gain * iw_ref[1:2, :]
    slope = (gw1 - gw0) * (1.0 / 16.0)
    slope_mean = jnp.mean(slope)
    base0 = jnp.sum(bias * iw_ref[0:1, :]) + ibias[0]
    base1 = jnp.sum(bias * iw_ref[1:2, :]) + ibias[1]
    part = 256
    tails = part // 16

    def tail(negative, m):
        first = m * part
        r = pl.ds(pl.multiple_of(first, 256), part)
        h = x[r, :].astype(F32) + mm(ctx[r, :], wo_ref[...], NN)
        center = h - jnp.mean(h, axis=-1, keepdims=True)
        spread = jnp.mean(center * center, axis=-1, keepdims=True)
        rstd = lax.rsqrt(spread + 1e-6)
        xhat = center * rstd
        a0 = jnp.sum(xhat * gw0, axis=-1, keepdims=True)
        a1 = jnp.sum(xhat * gw1, axis=-1, keepdims=True)
        l0 = jnp.mean(a0.reshape(tails, 16, 1), axis=1, keepdims=True) + base0
        l1 = jnp.mean(a1.reshape(tails, 16, 1), axis=1, keepdims=True) + base1
        sign = 1.0 if negative else -1.0
        g1 = sign / (1.0 + jnp.exp(-sign * (l1 - l0)))
        g1 = jnp.broadcast_to(g1, (tails, 16, 1)).reshape(part, 1)
        moved = (a1 - a0) * (1.0 / (16.0 * width))
        g = (rstd * g1) * ((slope - slope_mean) - xhat * moved)
        gh[r, :] = g
        low_g = g.astype(BF)
        ga[r, :] = low_g
        gc[r, :] = mm(low_g, wo_ref[...], NT).astype(BF)
        both = jnp.where(lax.broadcasted_iota(jnp.int32, (tails, 1, 128), 2) == 0, l0, l1)
        logits_ref[pl.ds(m * tails, tails)] = both

    def backward(negative, u):
        r, tr = spans(negative, u)
        heads = range(pairs_of_heads)
        cols = [slice(j * 128, (j + 1) * 128) for j in heads]
        gps = [mm(gc[r, c], keys_of(negative, u, j, 2 * width), NT) for j, c in zip(heads, cols)]
        both = []
        for j, gp in zip(heads, gps):
            p = prob[r, j * 256 : (j + 1) * 256]
            gs, lows = [], []
            for h in range(2):
                ph = p[:, h * 128 : (h + 1) * 128]
                gph = gp[:, h * 128 : (h + 1) * 128]
                mean = jnp.sum(gph * ph, axis=-1, keepdims=True)
                gs.append((ph * (gph - mean) * scale).astype(BF))
                lows.append(ph.astype(BF))
            both.append((gs, lows))
        gqs = [mm(jnp.concatenate(gs, axis=1), keys_of(negative, u, j, width), NN) for j, (gs, _) in zip(heads, both)]
        gks = [mm(jnp.concatenate(gs, axis=0), by_head(qkv[r, c]), TN) for c, (gs, _) in zip(cols, both)]
        gvs = [mm(jnp.concatenate(lows, axis=0), by_head(gc[r, c]), TN) for c, (_, lows) in zip(cols, both)]
        for j, c, gq, gk, gv in zip(heads, cols, gqs, gks, gvs):
            cv = slice(width + j * 128, width + (j + 1) * 128)
            gqkv[r, c] = gq.astype(BF)
            gqkv[r, cv] = gk[:64].astype(BF)
            gqkv[r, 2 * width + j * 128 : 2 * width + (j + 1) * 128] = gv[:64].astype(BF)
            if negative:
                gt[tr, c] = (gk[64:96] + gt_own[tr, c]).astype(BF)
                gt[tr, cv] = (gv[64:96] + gt_own[tr, cv]).astype(BF)
            else:
                gt_own[tr, c] = gk[64:]
                gt_own[tr, cv] = gv[64:]

    def loop(first, last, step):
        def body(i, _):
            step(i)
            return 0

        lax.fori_loop(first, last, body, 0)

    def to_rows(m):
        r = pl.ds(pl.multiple_of(m * part, 256), part)
        return mm(gqkv[r, :], w_ref[...], NT) + gh[r, :]

    x[0:own, :] = q_ref[...]
    loop(0, own // unit, lambda u: forward(False, u))

    @pl.when(holding)
    def _():
        pltpu.make_async_copy(held.at[core], held.at[core], held_sem).wait()
        swap_copy().start()
        lanes = lax.broadcasted_iota(jnp.int32, (slots, 128), 1)
        lines = lax.broadcasted_iota(jnp.int32, (slots, 128), 0)
        spot = lax.broadcasted_iota(jnp.int32, (1, 2048), 1)
        side, rest = lax.div(spot, 1024), lax.rem(spot, 1024)
        ids = ((lax.div(rest, 16) * 2 + side) * 16 + lax.rem(rest, 16) + 1).astype(F32)
        values = held.reshape(2048, PIECE)
        pltpu.make_async_copy(held.at[other], held.at[other], swap_recv).wait()

        def pick(g, _):
            columns = []
            for b in range(8):
                row = table[2 * (g * 8 + b) + core].astype(F32)
                eye = lanes == lines + 32 * (b % 4)
                columns.append(jnp.sum(jnp.where(eye, row, 0.0), axis=-1, keepdims=True))
            hot = one_hot(jnp.concatenate(columns, axis=0) == ids)
            chosen = mm(hot, values[...], NN).astype(BF)
            for b in range(8):
                to = g * 8 + b
                target = 2 * to + core
                picked[to] = chosen[b * slots : (b + 1) * slots]

                @pl.when(target != me)
                def _():
                    remote(picked.at[to], arrived.at[mine], pick_send, pick_sem, target).start()

                @pl.when(target == me)
                def _():
                    pltpu.make_async_copy(picked.at[to], arrived.at[mine], pick_sem).start()

            return 0

        lax.fori_loop(0, chips // 8, pick, 0)

    wo_copy.wait()
    loop(0, own // part, lambda m: tail(False, m))
    loop(0, own // unit, lambda u: backward(False, u))
    own_grad[...] = to_rows(0)

    swap = swap_rows(16, slots)
    pltpu.make_async_copy(arrived, arrived, pick_sem).wait()
    for k in range(3):
        c = slice(k * PIECE, (k + 1) * PIECE)
        stacked = jnp.concatenate([arrived[r * 3 + k] for r in range(16)], axis=0)
        x[own:rows, c] = mm(swap, stacked, NN).astype(BF)

    def negative_step(j):
        c = pl.ds(pl.multiple_of(j * col, col), col)
        qkv[own:rows, c] = mm(x[own:rows, :], w_ref[:, c], NN).astype(BF)

    loop(0, 3 * width // col, negative_step)
    loop(0, (rows - own) // unit, lambda u: forward(True, u))
    loop(own // part, rows // part, lambda m: tail(True, m))
    loop(0, (rows - own) // unit, lambda u: backward(True, u))

    def negative_rows(m):
        back[pl.ds(pl.multiple_of((m - 1) * part, 256), part), :] = to_rows(m).astype(BF)

    loop(own // part, rows // part, negative_rows)
    swapped = mm(swap_rows(slots, 16), back[...], NN).astype(BF)
    for r in range(16):
        for k in range(3):
            back_pieces[r * 3 + k] = swapped[r * slots : (r + 1) * slots, k * PIECE : (k + 1) * PIECE]

    def spread_back(i, _):
        piece = (i + me) % HOLDERS
        target = holder(piece, core)

        @pl.when(target != me)
        def _():
            remote(back_pieces.at[piece], back_held.at[chip], back_send, back_sem, target).start()

        @pl.when(target == me)
        def _():
            pltpu.make_async_copy(back_pieces.at[piece], back_held.at[chip], back_sem).start()

        return 0

    lax.fori_loop(0, HOLDERS, spread_back, 0)

    def half_copy(j):
        return remote(grads.at[j, twin_rows], half_in.at[j], half_send.at[j], half_recv.at[j], twin)

    def weight_step(j, _):
        c = pl.ds(pl.multiple_of(j * col, col), col)
        grads[j] = mm(x[...], gqkv[:, c], TN).astype(BF)
        half_copy(j).start()
        return 0

    lax.fori_loop(0, width // col, weight_step, 0)

    def weight_text_step(j, _):
        c = pl.ds(pl.multiple_of(j * col, col), col)
        ct = pl.ds(pl.multiple_of(j * col - width, col), col)
        grads[j] = (mm(x[...], gqkv[:, c], TN) + mm(t_ref[...], gt[:, ct], TN)).astype(BF)
        half_copy(j).start()
        return 0

    lax.fori_loop(width // col, 3 * width // col, weight_text_step, 0)

    def out_step(j, _):
        c = pl.ds(pl.multiple_of(j * col - 3 * width, col), col)
        grads[j] = mm(ctx[...], ga[:, c], TN).astype(BF)
        half_copy(j).start()
        return 0

    lax.fori_loop(3 * width // col, 4 * width // col, out_step, 0)

    sends = []

    def start(copy):
        copy.start()
        sends.append(copy)

    one = {}
    for t in thirds:
        axis = axis_of(t, 0)

        def add_half(k, _, t=t):
            half_copy(4 * t + k).wait_recv()
            own = grads[4 * t + k, mine_rows, :].astype(F32)
            half_in[4 * t + k] = (own + half_in[4 * t + k].astype(F32)).astype(BF)
            return 0

        lax.fori_loop(0, 4, add_half, 0)
        for d in (1, 2, 3):
            to = (spots[axis] + d) % 4
            one[t, d] = remote(half_in.at[4 * t + to], in1.at[t, d - 1],
                               s_send.at[t, d], s_recv.at[t, d], along(axis, d))
            start(one[t, d])

    def partial_copy():
        return remote(partial, twin_partial, partial_send, partial_recv, twin)

    @pl.when(holding)
    def _():
        pltpu.make_async_copy(back_held, back_held, back_sem).wait()
        values = back_held.reshape(chips * slots, PIECE)
        line_at = lax.broadcasted_iota(jnp.int32, (256, 128), 0)
        ids = (lax.div(line_at, 16) * 32 + lax.rem(line_at, 16) + 1).astype(F32)
        rows_of = [
            sum(table[2 * (4 * b + i) + core].astype(F32) for i in range(4)) for b in range(chips // 4)
        ]

        def total_of(g, side):
            shift = (g * 512 + side * 16).astype(F32)
            hot = jnp.concatenate([one_hot(ids == row - shift) for row in rows_of], axis=1)
            return mm(hot, values[...], NN)

        def for_twin(g, _):
            total = total_of(g, other).astype(BF)
            for b in range(16):
                partial[g * 16 + b] = total[b * images : (b + 1) * images]
            return 0

        lax.fori_loop(0, chips // 16, for_twin, 0)
        partial_copy().start()
        partial_copy().wait_recv()

        def add_up(g, _):
            more = twin_partial[pl.ds(g * 16, 16)].reshape(256, PIECE).astype(F32)
            total = (total_of(g, core) + more).astype(BF)
            for b in range(16):
                to = g * 16 + b
                target = 2 * to + core
                totals[to] = total[b * images : (b + 1) * images]

                @pl.when(target != me)
                def _():
                    remote(totals.at[to], back_arrived.at[mine], total_send, total_sem, target).start()

                @pl.when(target == me)
                def _():
                    pltpu.make_async_copy(totals.at[to], back_arrived.at[mine], total_sem).start()

            return 0

        lax.fori_loop(0, chips // 16, add_up, 0)

    gtext_ref[...] = mm(gt[...], w_ref[:, width:], NT).astype(BF)

    two = {}
    for t in thirds:
        axis, after = axis_of(t, 0), axis_of(t, 1)
        for d in (1, 2, 3):
            one[t, d].wait_recv()
        total = half_in[4 * t + spots[axis]].astype(F32)
        for d in range(3):
            total += in1[t, d].astype(F32)
        sum1[t] = total.astype(BF)
        for d in (1, 2, 3):
            to = (spots[after] + d) % 4
            two[t, d] = remote(sum1.at[t, pl.ds(pl.multiple_of(to * 96, 32), 96)], in2.at[t, d - 1],
                               s_send.at[t, 3 + d], s_recv.at[t, 3 + d], along(after, d))
            start(two[t, d])

    def corner(ref, first, spot):
        rows = pl.ds(pl.multiple_of(first + (spot // 2) * 48, 16), 48)
        return ref.at[rows, pl.ds(pl.multiple_of((spot % 2) * 128, 128), 128)]

    three = {}
    for t in thirds:
        axis, after = axis_of(t, 1), axis_of(t, 2)
        for d in (1, 2, 3):
            two[t, d].wait_recv()
        total = sum1[t, pl.ds(pl.multiple_of(spots[axis] * 96, 32), 96), :].astype(F32)
        for d in range(3):
            total += in2[t, d].astype(F32)
        sum2[t] = total.astype(BF)
        for d in (1, 2, 3):
            to = (spots[after] + d) % 4
            three[t, d] = remote(corner(sum2.at[t], 0, to), in3.at[t, d - 1],
                                 s_send.at[t, 6 + d], s_recv.at[t, 6 + d], along(after, d))
            start(three[t, d])

    last = {}
    for t in thirds:
        axis = axis_of(t, 2)
        for d in (1, 2, 3):
            three[t, d].wait_recv()
        total = corner(sum2.at[t], 0, spots[axis])[...].astype(F32)
        for d in range(3):
            total += in3[t, d].astype(F32)
        block = sum_ref.at[4 * t + spots[axis_of(t, 0)]]
        first = core * 384 + spots[axis_of(t, 1)] * 96
        piece = corner(block, first, spots[axis])
        piece[...] = total.astype(BF)
        for d in (1, 2, 3):
            last[t, d] = remote(piece, piece, a_send.at[t, d], a_recv.at[t, d], along(axis, d))
            start(last[t, d])

    def came(t, stage, ref, d):
        return pltpu.make_async_copy(ref, ref, a_recv.at[t, stage * 3 + d])

    for t in thirds:
        axis = axis_of(t, 1)
        block = sum_ref.at[4 * t + spots[axis_of(t, 0)]]
        first = core * 384 + spots[axis] * 96
        for d in (1, 2, 3):
            came(t, 0, corner(block, first, (spots[axis_of(t, 2)] + 4 - d) % 4), d).wait()
        piece = block.at[pl.ds(pl.multiple_of(first, 32), 96)]
        for d in (1, 2, 3):
            start(remote(piece, piece, a_send.at[t, 3 + d], a_recv.at[t, 3 + d], along(axis, d)))

    for t in thirds:
        axis = axis_of(t, 0)
        block = sum_ref.at[4 * t + spots[axis]]
        for d in (1, 2, 3):
            spot = (spots[axis_of(t, 1)] + 4 - d) % 4
            came(t, 1, block.at[pl.ds(pl.multiple_of(core * 384 + spot * 96, 32), 96)], d).wait()
        piece = block.at[mine_rows]
        start(remote(piece, piece, twin_send.at[t, 0], twin_recv.at[t, 0], twin))
        for d in (1, 2, 3):
            start(remote(piece, piece, a_send.at[t, 6 + d], a_recv.at[t, 6 + d], along(axis, d)))

    for t in thirds:
        axis = axis_of(t, 0)
        for d in (1, 2, 3):
            piece = sum_ref.at[4 * t + (spots[axis] + 4 - d) % 4, mine_rows]
            came(t, 2, piece, d).wait()
            start(remote(piece, piece, twin_send.at[t, d], twin_recv.at[t, d], twin))


    pltpu.make_async_copy(back_arrived, back_arrived, total_sem).wait()
    swap = swap_rows(16, images)
    for k in range(3):
        c = slice(k * PIECE, (k + 1) * PIECE)
        stacked = jnp.concatenate([back_arrived[r * 3 + k] for r in range(16)], axis=0)
        query_ref[:, c] = (own_grad[:, c] + mm(swap, stacked, NN)).astype(BF)

    for t in thirds:
        for d in range(4):
            late = sum_ref.at[4 * t + (spots[axis_of(t, 0)] + 4 - d) % 4, twin_rows]
            pltpu.make_async_copy(late, late, twin_recv.at[t, d]).wait()
    for copy in sends:
        copy.wait_send()

    def half_sent(j, _):
        half_copy(j).wait_send()
        return 0

    lax.fori_loop(0, 4 * width // col, half_sent, 0)

    def sent(ref, count, semaphore):
        pltpu.make_async_copy(ref.at[0:count], ref.at[0:count], semaphore).wait()

    for copy in gathers:
        copy.wait_send()

    @pl.when(holding)
    def _():
        swap_copy().wait_send()
        partial_copy().wait_send()
        sent(pieces, HOLDERS - 1, piece_send)
        sent(picked, chips - 1, pick_send)
        sent(back_pieces, HOLDERS - 1, back_send)
        sent(totals, chips - 1, total_send)

    @pl.when(jnp.logical_not(holding))
    def _():
        sent(pieces, HOLDERS, piece_send)
        sent(back_pieces, HOLDERS, back_send)


def pair_losses(lens, ib, need, queries, texts, w, wo, gain, bias, iw, peers):
    own, width = queries.shape
    rows, trows = 3 * own, texts.shape[0]
    images = own // 16
    vmem = pl.BlockSpec(memory_space=pltpu.VMEM)
    smem = pl.BlockSpec(memory_space=pltpu.SMEM)
    shape = jax.ShapeDtypeStruct
    dma = pltpu.SemaphoreType.DMA
    return pl.pallas_call(
        pair_kernel,
        out_shape=(
            shape((rows // 16, 1, 128), F32),
            shape((trows, width), BF),
            shape((own, width), BF),
            shape((12, width, 256), BF),
        ),
        in_specs=[smem, smem] + [vmem] * 3 + [pl.BlockSpec(memory_space=pl.ANY)] * 2 + [vmem] * 3,
        out_specs=(vmem,) * 4,
        scratch_shapes=[
            pltpu.VMEM((rows, width), BF),
            pltpu.VMEM((rows, 3 * width), BF),
            pltpu.VMEM((trows, 2 * width), BF),
            pltpu.VMEM((rows, width), BF),
            pltpu.VMEM((rows, width), F32),
            pltpu.VMEM((rows, width), BF),
            pltpu.VMEM((rows, width), BF),
            pltpu.VMEM((rows, 3 * width), BF),
            pltpu.VMEM((trows, 2 * width), BF),
            pltpu.VMEM((trows, 2 * width), F32),
            pltpu.VMEM((rows, 2 * width), F32),
            pltpu.VMEM((own, width), F32),
            pltpu.VMEM((2 * own, width), BF),
            pltpu.VMEM((12, width, 256), BF),
            pltpu.VMEM((peers, 1, 128), jnp.int32),
            pltpu.VMEM((HOLDERS, images, PIECE), BF),
            pltpu.VMEM((2, peers // 2, images, PIECE), BF),
            pltpu.VMEM((peers // 2, 2 * images, PIECE), BF),
            pltpu.VMEM((HOLDERS, 2 * images, PIECE), BF),
            pltpu.VMEM((HOLDERS, 2 * images, PIECE), BF),
            pltpu.VMEM((peers // 2, 2 * images, PIECE), BF),
            pltpu.VMEM((peers // 2, images, PIECE), BF),
            pltpu.VMEM((peers // 2, images, PIECE), BF),
            pltpu.VMEM((peers // 2, images, PIECE), BF),
            pltpu.VMEM((HOLDERS, images, PIECE), BF),
            pltpu.VMEM((12, 384, 256), BF),
            pltpu.VMEM((3, 3, 384, 256), BF),
            pltpu.VMEM((3, 384, 256), BF),
            pltpu.VMEM((3, 3, 96, 256), BF),
            pltpu.VMEM((3, 96, 256), BF),
            pltpu.VMEM((3, 3, 48, 128), BF),
            pltpu.VMEM((width, 3 * width), BF),
            pltpu.VMEM((width, width), BF),
            dma((2,)), dma((13,)), dma((13,)), dma, dma, dma, dma,
            dma, dma, dma, dma, dma, dma, dma, dma,
            dma((12,)), dma((12,)), dma((3, 10)), dma((3, 10)), dma((3, 10)), dma((3, 10)),
            dma((3, 4)), dma((3, 4)),
        ],
        compiler_params=pltpu.CompilerParams(
            vmem_limit_bytes=63 * 1024 * 1024, has_side_effects=True, collective_id=0
        ),
        name="pair_losses",
    )(lens, ib, need, queries, texts, w, wo, gain, bias, iw.T)


def widen_kernel(share, sum_ref, qkv_ref, out_ref):
    for j in range(12):
        block = sum_ref[j].astype(F32) * share
        if j < 9:
            qkv_ref[:, j * 256 : (j + 1) * 256] = block
        else:
            out_ref[:, (j - 9) * 256 : (j - 8) * 256] = block


def widen(sums, share):
    width, part = sums.shape[1], 96
    return pl.pallas_call(
        lambda *refs: widen_kernel(share, *refs),
        grid=(width // part,),
        out_shape=(
            jax.ShapeDtypeStruct((width, 3 * width), F32),
            jax.ShapeDtypeStruct((width, width), F32),
        ),
        in_specs=[pl.BlockSpec((12, part, 256), lambda j: (0, j, 0))],
        out_specs=(
            pl.BlockSpec((part, 3 * width), lambda j: (j, 0)),
            pl.BlockSpec((part, width), lambda j: (j, 0)),
        ),
        name="widen",
    )(sums)


def on_device(
    text_states, text_len, query_states, neg_owner, neg_slot,
    projection_weight, output_weight, ln_gain, ln_bias, itm_weight, itm_bias,
):
    captions, query_rows, width = query_states.shape
    peers = lax.axis_size("dp")
    me = lax.axis_index("dp")
    wanted = (captions * neg_owner + neg_slot + 1).reshape(1, 2 * captions)
    group = jnp.arange(4)[:, None] == me // 2 % 4
    need = jnp.where(group, wanted, 0).reshape(1, 128)
    logits, grad_text, grad_query, sums = pair_losses(
        text_len, itm_bias, need, query_states.reshape(-1, width), text_states.reshape(-1, width),
        projection_weight, output_weight, ln_gain, ln_bias, itm_weight, peers,
    )
    sum_qkv, sum_out = widen(sums, 1.0 / (captions * peers))
    return (
        jnp.concatenate(
            [logits[:captions, 0, :2].reshape(captions, 1, 2), logits[captions:, 0, :2].reshape(captions, 2, 2)],
            axis=1,
        ),
        grad_text.reshape(text_states.shape),
        grad_query.reshape(query_states.shape),
        sum_qkv,
        sum_out,
    )


def solution(mesh):
    rows = P("dp", None, None)
    placed = (rows, P("dp"), rows, P("dp", None), P("dp", None)) + (P(),) * 6
    return jax.shard_map(
        on_device, mesh=mesh, in_specs=placed, out_specs=(rows, rows, rows, P(), P()), check_vma=False
    )
```

time: 166 us -> 136 us (0.82)
  Pallas kernels: 161 us -> 130 us
    pallas_call x1, Pallas kernels: 151 us -> 122 us  [pair_losses(): pl.pallas_call(pair_kernel, out_shape=(shape((rows // 16, 1, 128), F32),...]
    pallas_call x1, Pallas kernels: 9.68 us -> 7.57 us  [widen(): pl.pallas_call(lambda *refs: widen_kernel(share, *refs), grid=(width // p...]
where the time goes in v4:
time: 136 us
  Pallas kernels  130 us (96%)
  local copies, waits for them, and re-layouts  3.93 us (3%)
  other arithmetic  1.37 us (1%)
    pallas_call x1, Pallas kernels, pair_losses(): pl.pallas_call(pair_kernel, out_shape=(shape((rows // 16, 1, 128), F32),...  122 us
    pallas_call x1, Pallas kernels, widen(): pl.pallas_call(lambda *refs: widen_kernel(share, *refs), grid=(width // p...  7.57 us

profile of v4, /device:TPU:1, one launch (start us, length us, event | category | flops | bytes accessed | tf_op | source)
XLA Modules:
  0.0 135.8 jit_solution(1009822952865122041)
XLA Ops:
  0.7 0.7 add_add_fusion
  1.4 0.1 copy.24
  1.5 0.1 broadcast_in_dim.24
  1.5 0.1 broadcast_select_fusion
  1.6 0.6 select_n.28.need_ref
  2.2 122.3 %pair_losses.1 = (f32[48,1,128]{2,1,0:T(1,128)}, bf16[256,768]{1,0:T(8,128)(2,1)}, bf16[256,768]{1,0:T(8,128)(2,1)}, bf16[12,768,256]{2,1,0:T(8,128)(2,1)}) custom-call(s32[16]{0:T(128)} %lens.1, f32[2]{0:T(128)} %ibias.1, s32[1,128]{1,0:T(1,128)} %select_n.28.need_ref, bf16[256,768]{1,0:T(8,128)(2,1)} %bitcast.6, bf16[256,768]{1,0:T(8,128)(2,1)} %bitcast.7, ...), custom_call_target="tpu_custom_call" | custom-call | tf_op jit(solution)/shard_map/pair_losses/pallas_call | solution.py:633
  124.5 0.0 copy-start.1
  124.5 0.0 copy-start
  124.5 0.8 slice.6
  125.3 0.7 slice.7
  126.0 0.1 copy.26
  126.1 0.1 copy.27
  126.2 0.6 pad_maximum_fusion
  126.8 7.6 %widen.1 = (f32[768,2304]{1,0:T(8,128)}, f32[768,768]{1,0:T(8,128)}) custom-call(bf16[12,768,256]{2,1,0:T(8,128)(2,1)} %get-tuple-element.14.refs_0_), custom_call_target="tpu_custom_call" | custom-call | tf_op jit(solution)/shard_map/widen/pallas_call | solution.py:700
  134.3 0.0 copy-done.1
  134.3 0.7 copy.32
  135.1 0.0 copy-done
  135.1 0.7 copy.33
  (1 shorter events, 0.0 us)
Async XLA Ops:
  124.5 9.8 %copy-start.1 = (bf16[256,768]{1,0:T(8,128)(2,1)S(1)}, bf16[256,768]{1,0:T(8,128)(2,1)}, u32[]{:S(2)}) copy-start(bf16[256,768]{1,0:T(8,128)(2,1)} %get-tuple-element.12) | copy-start | bytes 1179652
  124.5 10.6 %copy-start = (bf16[256,768]{1,0:T(8,128)(2,1)S(1)}, bf16[256,768]{1,0:T(8,128)(2,1)}, u32[]{:S(2)}) copy-start(bf16[256,768]{1,0:T(8,128)(2,1)} %get-tuple-element.13) | copy-start | bytes 1179652

commit v5 on v4

--- a/solution.py
+++ b/solution.py
@@ -201,8 +201,7 @@
             parts.append(jnp.zeros((32, 128), BF))
         return by_head(jnp.concatenate(parts, axis=0))
 
-    def forward(negative, u):
-        r, _ = spans(negative, u)
+    def mask_of(negative, u):
         rowi = lax.broadcasted_iota(jnp.int32, (unit, 128), 0)
         lanei = lax.broadcasted_iota(jnp.int32, (unit, 128), 1)
         block = rowi - lax.rem(rowi, 16)
@@ -217,23 +216,28 @@
                 jnp.where(rowi < 16, lens[4 * u], lens[4 * u + 1]),
                 jnp.where(rowi < 48, lens[4 * u + 2], lens[4 * u + 3]),
             )
-        valid = ((lanei >= block) & (lanei < block + 16)) | ((lanei >= start) & (lanei < start + live))
-        heads = range(pairs_of_heads)
+        return ((lanei >= block) & (lanei < block + 16)) | ((lanei >= start) & (lanei < start + live))
+
+    def forward(negative, v):
+        us = (2 * v, 2 * v + 1)
+        heads = [(i, j) for i in range(2) for j in range(pairs_of_heads)]
+        rs = [spans(negative, u)[0] for u in us]
+        valid = [mask_of(negative, u) for u in us]
         scores = [
-            mm(qkv[r, j * 128 : (j + 1) * 128], keys_of(negative, u, j, width), NT) * scale for j in heads
+            mm(qkv[rs[u], j * 128 : (j + 1) * 128], keys_of(negative, us[u], j, width), NT) * scale for u, j in heads
         ]
         probs = []
-        for s in scores:
+        for (u, _), s in zip(heads, scores):
             parts = []
             for h in range(2):
-                sh = jnp.where(valid, s[:, h * 128 : (h + 1) * 128], -1e30)
+                sh = jnp.where(valid[u], s[:, h * 128 : (h + 1) * 128], -1e30)
                 e = jnp.exp(sh - jnp.max(sh, axis=-1, keepdims=True))
                 parts.append(e * (1.0 / jnp.sum(e, axis=-1, keepdims=True)))
             probs.append(jnp.concatenate(parts, axis=1))
-        outs = [mm(p.astype(BF), keys_of(negative, u, j, 2 * width), NN) for j, p in zip(heads, probs)]
-        for j, p, o in zip(heads, probs, outs):
-            prob[r, j * 256 : (j + 1) * 256] = p
-            ctx[r, j * 128 : (j + 1) * 128] = o.astype(BF)
+        outs = [mm(p.astype(BF), keys_of(negative, us[u], j, 2 * width), NN) for (u, j), p in zip(heads, probs)]
+        for (u, j), p, o in zip(heads, probs, outs):
+            prob[rs[u], j * 256 : (j + 1) * 256] = p
+            ctx[rs[u], j * 128 : (j + 1) * 128] = o.astype(BF)
 
     gain = gain_ref[...].reshape(1, -1)
     bias = bias_ref[...].reshape(1, -1)
@@ -270,14 +274,16 @@
         both = jnp.where(lax.broadcasted_iota(jnp.int32, (tails, 1, 128), 2) == 0, l0, l1)
         logits_ref[pl.ds(m * tails, tails)] = both
 
-    def backward(negative, u):
-        r, tr = spans(negative, u)
-        heads = range(pairs_of_heads)
-        cols = [slice(j * 128, (j + 1) * 128) for j in heads]
-        gps = [mm(gc[r, c], keys_of(negative, u, j, 2 * width), NT) for j, c in zip(heads, cols)]
+    def backward(negative, v):
+        us = (2 * v, 2 * v + 1)
+        heads = [(i, j) for i in range(2) for j in range(pairs_of_heads)]
+        rs = [spans(negative, u)[0] for u in us]
+        trs = [spans(negative, u)[1] for u in us]
+        cols = [slice(j * 128, (j + 1) * 128) for _, j in heads]
+        gps = [mm(gc[rs[u], c], keys_of(negative, us[u], j, 2 * width), NT) for (u, j), c in zip(heads, cols)]
         both = []
-        for j, gp in zip(heads, gps):
-            p = prob[r, j * 256 : (j + 1) * 256]
+        for (u, j), gp in zip(heads, gps):
+            p = prob[rs[u], j * 256 : (j + 1) * 256]
             gs, lows = [], []
             for h in range(2):
                 ph = p[:, h * 128 : (h + 1) * 128]
@@ -286,10 +292,20 @@
                 gs.append((ph * (gph - mean) * scale).astype(BF))
                 lows.append(ph.astype(BF))
             both.append((gs, lows))
-        gqs = [mm(jnp.concatenate(gs, axis=1), keys_of(negative, u, j, width), NN) for j, (gs, _) in zip(heads, both)]
-        gks = [mm(jnp.concatenate(gs, axis=0), by_head(qkv[r, c]), TN) for c, (gs, _) in zip(cols, both)]
-        gvs = [mm(jnp.concatenate(lows, axis=0), by_head(gc[r, c]), TN) for c, (_, lows) in zip(cols, both)]
-        for j, c, gq, gk, gv in zip(heads, cols, gqs, gks, gvs):
+        gqs = [
+            mm(jnp.concatenate(gs, axis=1), keys_of(negative, us[u], j, width), NN)
+            for (u, j), (gs, _) in zip(heads, both)
+        ]
+        gks = [
+            mm(jnp.concatenate(gs, axis=0), by_head(qkv[rs[u], c]), TN)
+            for (u, _), c, (gs, _) in zip(heads, cols, both)
+        ]
+        gvs = [
+            mm(jnp.concatenate(lows, axis=0), by_head(gc[rs[u], c]), TN)
+            for (u, _), c, (_, lows) in zip(heads, cols, both)
+        ]
+        for (u, j), c, gq, gk, gv in zip(heads, cols, gqs, gks, gvs):
+            r, tr = rs[u], trs[u]
             cv = slice(width + j * 128, width + (j + 1) * 128)
             gqkv[r, c] = gq.astype(BF)
             gqkv[r, cv] = gk[:64].astype(BF)
@@ -313,7 +329,7 @@
         return mm(gqkv[r, :], w_ref[...], NT) + gh[r, :]
 
     x[0:own, :] = q_ref[...]
-    loop(0, own // unit, lambda u: forward(False, u))
+    loop(0, own // (2 * unit), lambda v: forward(False, v))
 
     @pl.when(holding)
     def _():
@@ -354,7 +370,7 @@
 
     wo_copy.wait()
     loop(0, own // part, lambda m: tail(False, m))
-    loop(0, own // unit, lambda u: backward(False, u))
+    loop(0, own // (2 * unit), lambda v: backward(False, v))
     own_grad[...] = to_rows(0)
 
     swap = swap_rows(16, slots)
@@ -369,9 +385,9 @@
         qkv[own:rows, c] = mm(x[own:rows, :], w_ref[:, c], NN).astype(BF)
 
     loop(0, 3 * width // col, negative_step)
-    loop(0, (rows - own) // unit, lambda u: forward(True, u))
+    loop(0, (rows - own) // (2 * unit), lambda v: forward(True, v))
     loop(own // part, rows // part, lambda m: tail(True, m))
-    loop(0, (rows - own) // unit, lambda u: backward(True, u))
+    loop(0, (rows - own) // (2 * unit), lambda v: backward(True, v))
 
     def negative_rows(m):
         back[pl.ds(pl.multiple_of((m - 1) * part, 256), part), :] = to_rows(m).astype(BF)
@@ -475,27 +491,6 @@
 
         lax.fori_loop(0, chips // 16, for_twin, 0)
         partial_copy().start()
-        partial_copy().wait_recv()
-
-        def add_up(g, _):
-            more = twin_partial[pl.ds(g * 16, 16)].reshape(256, PIECE).astype(F32)
-            total = (total_of(g, core) + more).astype(BF)
-            for b in range(16):
-                to = g * 16 + b
-                target = 2 * to + core
-                totals[to] = total[b * images : (b + 1) * images]
-
-                @pl.when(target != me)
-                def _():
-                    remote(totals.at[to], back_arrived.at[mine], total_send, total_sem, target).start()
-
-                @pl.when(target == me)
-                def _():
-                    pltpu.make_async_copy(totals.at[to], back_arrived.at[mine], total_sem).start()
-
-            return 0
-
-        lax.fori_loop(0, chips // 16, add_up, 0)
 
     gtext_ref[...] = mm(gt[...], w_ref[:, width:], NT).astype(BF)
 
@@ -572,6 +567,41 @@
         start(remote(piece, piece, twin_send.at[t, 0], twin_recv.at[t, 0], twin))
         for d in (1, 2, 3):
             start(remote(piece, piece, a_send.at[t, 6 + d], a_recv.at[t, 6 + d], along(axis, d)))
+
+    @pl.when(holding)
+    def _():
+        partial_copy().wait_recv()
+        values = back_held.reshape(chips * slots, PIECE)
+        line_at = lax.broadcasted_iota(jnp.int32, (256, 128), 0)
+        ids = (lax.div(line_at, 16) * 32 + lax.rem(line_at, 16) + 1).astype(F32)
+        rows_of = [
+            sum(table[2 * (4 * b + i) + core].astype(F32) for i in range(4)) for b in range(chips // 4)
+        ]
+
+        def total_of(g, side):
+            shift = (g * 512 + side * 16).astype(F32)
+            hot = jnp.concatenate([one_hot(ids == row - shift) for row in rows_of], axis=1)
+            return mm(hot, values[...], NN)
+
+        def add_up(g, _):
+            more = twin_partial[pl.ds(g * 16, 16)].reshape(256, PIECE).astype(F32)
+            total = (total_of(g, core) + more).astype(BF)
+            for b in range(16):
+                to = g * 16 + b
+                target = 2 * to + core
+                totals[to] = total[b * images : (b + 1) * images]
+
+                @pl.when(target != me)
+                def _():
+                    remote(totals.at[to], back_arrived.at[mine], total_send, total_sem, target).start()
+
+                @pl.when(target == me)
+                def _():
+                    pltpu.make_async_copy(totals.at[to], back_arrived.at[mine], total_sem).start()
+
+            return 0
+
+        lax.fori_loop(0, chips // 16, add_up, 0)
 
     for t in thirds:
         axis = axis_of(t, 0)

time: 136 us -> 133 us (0.978)
  Pallas kernels: 130 us -> 127 us
    pallas_call x1, Pallas kernels: 122 us -> 119 us  [pair_losses(): pl.pallas_call(pair_kernel, out_shape=(shape((rows // 16, 1, 128), F32),...]
where the time goes in v5:
time: 133 us
  Pallas kernels  127 us (95%)
  local copies, waits for them, and re-layouts  3.93 us (3%)
  other arithmetic  1.37 us (1%)
    pallas_call x1, Pallas kernels, pair_losses(): pl.pallas_call(pair_kernel, out_shape=(shape((rows // 16, 1, 128), F32),...  119 us
    pallas_call x1, Pallas kernels, widen(): pl.pallas_call(lambda *refs: widen_kernel(share, *refs), grid=(width // p...  7.57 us

profile of v5, /device:TPU:1, one launch (start us, length us, event | category | flops | bytes accessed | tf_op | source)
XLA Modules:
  0.0 132.7 jit_solution(4930103030226742081)
XLA Ops:
  0.7 0.7 add_add_fusion
  1.4 0.1 copy.24
  1.5 0.1 broadcast_in_dim.24
  1.5 0.1 broadcast_select_fusion
  1.6 0.6 select_n.28.need_ref
  2.2 119.1 %pair_losses.1 = (f32[48,1,128]{2,1,0:T(1,128)}, bf16[256,768]{1,0:T(8,128)(2,1)}, bf16[256,768]{1,0:T(8,128)(2,1)}, bf16[12,768,256]{2,1,0:T(8,128)(2,1)}) custom-call(s32[16]{0:T(128)} %lens.1, f32[2]{0:T(128)} %ibias.1, s32[1,128]{1,0:T(1,128)} %select_n.28.need_ref, bf16[256,768]{1,0:T(8,128)(2,1)} %bitcast.6, bf16[256,768]{1,0:T(8,128)(2,1)} %bitcast.7, ...), custom_call_target="tpu_custom_call" | custom-call | tf_op jit(solution)/shard_map/pair_losses/pallas_call | solution.py:663
  121.4 0.0 copy-start.1
  121.4 0.0 copy-start
  121.4 0.8 slice.6
  122.2 0.7 slice.7
  122.9 0.1 copy.26
  123.0 0.1 copy.27
  123.0 0.6 pad_maximum_fusion
  123.6 7.6 %widen.1 = (f32[768,2304]{1,0:T(8,128)}, f32[768,768]{1,0:T(8,128)}) custom-call(bf16[12,768,256]{2,1,0:T(8,128)(2,1)} %get-tuple-element.14.refs_0_), custom_call_target="tpu_custom_call" | custom-call | tf_op jit(solution)/shard_map/widen/pallas_call | solution.py:730
  131.2 0.0 copy-done.1
  131.2 0.7 copy.32
  132.0 0.0 copy-done
  132.0 0.7 copy.33
  (1 shorter events, 0.0 us)
Async XLA Ops:
  121.4 9.8 %copy-start.1 = (bf16[256,768]{1,0:T(8,128)(2,1)S(1)}, bf16[256,768]{1,0:T(8,128)(2,1)}, u32[]{:S(2)}) copy-start(bf16[256,768]{1,0:T(8,128)(2,1)} %get-tuple-element.12) | copy-start | bytes 1179652
  121.4 10.6 %copy-start = (bf16[256,768]{1,0:T(8,128)(2,1)S(1)}, bf16[256,768]{1,0:T(8,128)(2,1)}, u32[]{:S(2)}) copy-start(bf16[256,768]{1,0:T(8,128)(2,1)} %get-tuple-element.13) | copy-start | bytes 1179652

commit v6 on v5

--- a/solution.py
+++ b/solution.py
@@ -726,7 +726,7 @@
 
 
 def widen(sums, share):
-    width, part = sums.shape[1], 96
+    width, part = sums.shape[1], 192
     return pl.pallas_call(
         lambda *refs: widen_kernel(share, *refs),
         grid=(width // part,),
@@ -739,6 +739,7 @@
             pl.BlockSpec((part, 3 * width), lambda j: (j, 0)),
             pl.BlockSpec((part, width), lambda j: (j, 0)),
         ),
+        compiler_params=pltpu.CompilerParams(vmem_limit_bytes=32 * 1024 * 1024),
         name="widen",
     )(sums)
 

time: 133 us -> 132 us (level)
  Pallas kernels: 127 us -> 123 us
  local copies, waits for them, and re-layouts: 3.93 us -> 6.2 us
    pallas_call x1, Pallas kernels: 7.57 us -> 3.94 us  [widen(): pl.pallas_call(lambda *refs: widen_kernel(share, *refs), grid=(width // p...]
    unnamed x6 -> x8, local copies, waits for them, and re-layouts: 1.5 us -> 3.84 us
where the time goes in v6:
time: 132 us; the launch traced here: 131 us
  Pallas kernels  123 us (93%)
  local copies, waits for them, and re-layouts  6.2 us (5%)
  other arithmetic  1.37 us (1%)
    pallas_call x1, Pallas kernels, pair_losses(): pl.pallas_call(pair_kernel, out_shape=(shape((rows // 16, 1, 128), F32),...  119 us
    pallas_call x1, Pallas kernels, widen(): pl.pallas_call(lambda *refs: widen_kernel(share, *refs), grid=(width // p...  3.94 us
    unnamed x8, local copies, waits for them, and re-layouts  3.84 us

profile of v6, /device:TPU:1, one launch (start us, length us, event | category | flops | bytes accessed | tf_op | source)
XLA Modules:
  0.0 131.3 jit_solution(230008484336752308)
XLA Ops:
  0.7 0.7 add_add_fusion
  1.4 0.1 copy.24
  1.5 0.1 broadcast_in_dim.24
  1.5 0.1 broadcast_select_fusion
  1.6 0.6 select_n.28.need_ref
  2.2 119.1 %pair_losses.1 = (f32[48,1,128]{2,1,0:T(1,128)}, bf16[256,768]{1,0:T(8,128)(2,1)}, bf16[256,768]{1,0:T(8,128)(2,1)}, bf16[12,768,256]{2,1,0:T(8,128)(2,1)}) custom-call(s32[16]{0:T(128)} %lens.1, f32[2]{0:T(128)} %ibias.1, s32[1,128]{1,0:T(1,128)} %select_n.28.need_ref, bf16[256,768]{1,0:T(8,128)(2,1)} %bitcast.6, bf16[256,768]{1,0:T(8,128)(2,1)} %bitcast.7, ...), custom_call_target="tpu_custom_call" | custom-call | tf_op jit(solution)/shard_map/pair_losses/pallas_call | solution.py:663
  121.4 0.7 slice.6
  122.1 0.7 slice.7
  122.8 0.1 copy.26
  122.9 0.1 copy.27
  123.0 0.6 pad_maximum_fusion
  123.5 0.0 copy-start
  123.5 2.3 %copy-done = bf16[12,768,256]{2,1,0:T(8,128)(2,1)S(1)} copy-done((bf16[12,768,256]{2,1,0:T(8,128)(2,1)S(1)}, bf16[12,768,256]{2,1,0:T(8,128)(2,1)}, u32[]{:S(2)}) %copy-start) | copy-done | bytes 4718616
  125.9 0.0 copy-start.2
  125.9 0.0 copy-start.1
  125.9 3.9 %widen.1 = (f32[768,2304]{1,0:T(8,128)}, f32[768,768]{1,0:T(8,128)}) custom-call(bf16[12,768,256]{2,1,0:T(8,128)(2,1)S(1)} %copy-done), custom_call_target="tpu_custom_call" | custom-call | tf_op jit(solution)/shard_map/widen/pallas_call | solution.py:730
  129.8 0.0 copy-done.2
  129.8 0.7 copy.32
  130.6 0.0 copy-done.1
  130.6 0.7 copy.33
  (1 shorter events, 0.0 us)
Async XLA Ops:
  123.5 2.3 %copy-start = (bf16[12,768,256]{2,1,0:T(8,128)(2,1)S(1)}, bf16[12,768,256]{2,1,0:T(8,128)(2,1)}, u32[]{:S(2)}) copy-start(bf16[12,768,256]{2,1,0:T(8,128)(2,1)} %get-tuple-element.14.refs_0_) | copy-start | bytes 14155780
  125.9 3.9 %copy-start.2 = (bf16[256,768]{1,0:T(8,128)(2,1)S(1)}, bf16[256,768]{1,0:T(8,128)(2,1)}, u32[]{:S(2)}) copy-start(bf16[256,768]{1,0:T(8,128)(2,1)} %get-tuple-element.12) | copy-start | bytes 1179652
  125.9 4.7 %copy-start.1 = (bf16[256,768]{1,0:T(8,128)(2,1)S(1)}, bf16[256,768]{1,0:T(8,128)(2,1)}, u32[]{:S(2)}) copy-start(bf16[256,768]{1,0:T(8,128)(2,1)} %get-tuple-element.13) | copy-start | bytes 1179652
